TPU v7x, 512 devices: a whole 4x8x8 slice. The times are simulated.
512 devices in a mesh: tr: 8 (over y), tc: 4 (over z_lo), ga: 16 (over x, z_hi, core).
Axes of the slice: x: 4, y: 8, z: 8 (z_hi: 2, z_lo: 4; z = z_hi * 4 + z_lo), core: 2. Of those that a mesh axis runs over, the one named last changes fastest.
Arguments:
- valence: bfloat16 [2, 16, 64, 4096], P(None, None, 'ga'), may hold values from -6 to 6
- conduction: bfloat16 [2, 16, 64, 4096], P(None, None, 'ga'), may hold values from -6 to 6
- envelope: bfloat16 [2, 64, 4096], P(None, 'ga'), may hold values from -6 to 6
- valence_index: int32 [256], P(('tr', 'tc')), may hold values from 0 to 15, as said below
- conduction_index: int32 [256], P(('tr', 'tc')), may hold values from 0 to 15, as said below
- grid_index: int32 [10240], replicated, may hold values from 0 to 262143, as said below
- coulomb: float32 [10240], P('ga'), may hold values from 0.1 to 10
Outputs:
- kernel_panel: float32 [2, 256, 256], P(None, ('tr', 'tc'), 'ga')
Inputs may be any that keep to these rules, and one draw needn't show every extreme that they name: `grid_index`: entries are distinct; block k of 640 entries (entries k * 640 to (k + 1) * 640 - 1) has ky in k * 4 to (k + 1) * 4 - 1. `valence_index`: valence_index[t] * 16 + conduction_index[t] takes each value of 0 to 255 once, so every pair of a valence band and a conduction band stands at exactly one transition. `conduction_index`: together with valence_index, every pair of a valence band and a conduction band stands at exactly one transition.
All inputs are finite; a program needn't handle non-finite values.
Results may differ from a plain program's by a relative error of at most 0.0005.
Values may be sent and summed in bfloat16 or wider, within the bound.
No kernel may reach another device: no remote copies, remote signals or barrier semaphores. Data moves between devices by JAX's collectives and lax.ppermute only.
A program may use at most 192 MiB of HBM per device.

v0:
```python
import math

import jax
import jax.numpy as jnp
from jax import lax
from jax.sharding import PartitionSpec as P

precise = lax.Precision.HIGHEST


def twiddle(products, points):
    angles = products.astype(jnp.float32) * (2.0 * math.pi / points)
    return (jnp.cos(angles), jnp.sin(angles))


def section(real_part, imag_part, form, points):
    indices = lax.iota(jnp.int32, points)
    cosine, sine = twiddle(indices[:, None] * indices[None, :] % points, points)
    factor = 1.0 / math.sqrt(points)
    real_out = jnp.einsum(form, real_part, cosine, precision=precise) + jnp.einsum(
        form, imag_part, sine, precision=precise
    )
    imag_out = jnp.einsum(form, imag_part, cosine, precision=precise) - jnp.einsum(
        form, real_part, sine, precision=precise
    )
    return (real_out * factor, imag_out * factor)


def plane_sum(data_real, data_imag, planes, wave_x, columns, points):
    picked_real = jnp.take(data_real, columns, axis=2)
    picked_imag = jnp.take(data_imag, columns, axis=2)
    cosine, sine = twiddle(planes[:, None] * wave_x[None, :] % points, points)
    factor = 1.0 / math.sqrt(points)
    real_out = jnp.einsum("txg,xg->tg", picked_real, cosine, precision=precise) + jnp.einsum(
        "txg,xg->tg", picked_imag, sine, precision=precise
    )
    imag_out = jnp.einsum("txg,xg->tg", picked_imag, cosine, precision=precise) - jnp.einsum(
        "txg,xg->tg", picked_real, sine, precision=precise
    )
    return (real_out * factor, imag_out * factor)


def body(valence, conduction, envelope, valence_index, conduction_index, grid_index, coulomb):
    points = math.isqrt(valence.shape[-1])
    thickness = valence.shape[2]
    local_count = valence_index.shape[0]
    valence_rows = jnp.take(valence, valence_index, axis=1).astype(jnp.float32)
    conduct_rows = (
        jnp.take(conduction, conduction_index, axis=1).astype(jnp.float32)
        + envelope.astype(jnp.float32)[:, None]
    )
    real_part = valence_rows[0] * conduct_rows[0] + valence_rows[1] * conduct_rows[1]
    imag_part = valence_rows[0] * conduct_rows[1] - valence_rows[1] * conduct_rows[0]
    real_part = real_part.reshape(local_count, thickness, points, points)
    imag_part = imag_part.reshape(local_count, thickness, points, points)
    real_part, imag_part = section(real_part, imag_part, "tpyz,zk->tpyk", points)
    real_part, imag_part = section(real_part, imag_part, "tpyz,yk->tpkz", points)
    position = lax.axis_index("ga")
    groups = lax.axis_size("ga")
    per_device = coulomb.shape[0]
    stacked = jnp.stack([real_part, imag_part])
    moved = lax.all_to_all(stacked, "ga", split_axis=3, concat_axis=2, tiled=True)
    flat = moved.reshape(2, local_count, points, thickness * points)
    local_ids = lax.dynamic_slice_in_dim(grid_index, position * per_device, per_device)
    wave_x = local_ids // (points * points)
    wave_y = local_ids // points % points - position * thickness
    wave_z = local_ids % points
    columns = wave_y * points + wave_z
    planes = lax.iota(jnp.int32, points)
    real_out, imag_out = plane_sum(flat[0], flat[1], planes, wave_x, columns, points)
    spectrum = jnp.stack([real_out, imag_out])
    weighted = (spectrum * jnp.sqrt(coulomb)[None, None, :]).astype(jnp.bfloat16)
    inverse = 1.0 / (per_device * groups)
    contract = (((1,), (1,)), ((), ()))
    piece = lax.all_gather(weighted, ("tr", "tc"), axis=1, tiled=True)
    left_real = weighted[0]
    left_imag = weighted[1]
    right_real = piece[0]
    right_imag = piece[1]
    kernel_real = lax.dot_general(
        left_real, right_real, contract, preferred_element_type=jnp.float32
    ) + lax.dot_general(left_imag, right_imag, contract, preferred_element_type=jnp.float32)
    kernel_imag = lax.dot_general(
        left_real, right_imag, contract, preferred_element_type=jnp.float32
    ) - lax.dot_general(left_imag, right_real, contract, preferred_element_type=jnp.float32)
    terms = jnp.stack([kernel_real, kernel_imag]) * inverse
    return lax.psum_scatter(terms, "ga", scatter_dimension=2, tiled=True)


def solution(mesh):
    placed = (
        P(None, None, "ga", None),
        P(None, None, "ga", None),
        P(None, "ga", None),
        P(("tr", "tc")),
        P(("tr", "tc")),
        P(),
        P("ga"),
    )
    return jax.shard_map(
        body, mesh=mesh, in_specs=placed, out_specs=P(None, ("tr", "tc"), "ga"), check_vma=False
    )
```

profile of v0, /device:TPU:1, one launch (start us, length us, event | category | flops | bytes accessed | tf_op | source)
XLA Modules:
  0.0 275.2 jit_solution(5719047248334247920)
XLA Ops:
  11.2 2.2 gather_fusion
  14.0 1.1 multiply_add_fusion
  15.6 2.1 fusion.26
  17.7 1.6 sub.39
  21.6 1.2 fusion.30
  23.9 1.2 fusion.28
  25.1 1.2 fusion.7
  26.3 1.4 fusion.5
  27.9 1.4 copy.88
  29.3 2.9 %reshape.95 = f32[16,1,16384]{2,1,0:T(1,128)} reshape(f32[64,2,8,4,64]{4,3,2,1,0:T(4,128)S(1)} %bitcast.117) | data formatting | bytes 2097152
  32.2 14.3 %all-to-all-start = ((f32[16,1,16384]{2,1,0:T(1,128)}), f32[16,1,16384]{2,1,0:T(1,128)S(1)}, u32[]{:S(2)}, u32[]{:S(2)}) async-start(f32[16,1,16384]{2,1,0:T(1,128)} %reshape.95), calls=%async_computation | async-start | bytes 2097152 | tf_op jit(solution)/shard_map/all_to_all | solution.py:62
  49.8 16.5 %all-to-all-done = f32[16,1,16384]{2,1,0:T(1,128)S(1)} async-done(((f32[16,1,16384]{2,1,0:T(1,128)}), f32[16,1,16384]{2,1,0:T(1,128)S(1)}, u32[]{:S(2)}, u32[]{:S(2)}) %all-to-all-start) | async-done | bytes 1048608 | tf_op jit(solution)/shard_map/all_to_all | solution.py:62
  66.8 4.4 %reduce.8 = f32[16,16384]{1,0:T(8,128)} reduce(f32[16,1,16384]{2,1,0:T(1,128)S(1)} %all-to-all-done, f32[]{:T(128)} %broadcast.223), dimensions={1}, to_apply=%all_to_all.11.reduce_sub_computation | reduce | bytes 2097156 | tf_op jit(solution)/shard_map/all_to_all | solution.py:62
  71.2 2.6 reshape.96
  73.9 1.4 copy.87
  75.7 1.4 squeeze.13
  77.1 1.5 copy.35
  78.6 1.4 squeeze.12
  80.0 1.5 copy.34
  81.5 3.6 %gather_fusion.3 = f32[640,8,64]{2,1,0:T(8,128)} fusion(f32[8,64,256]{1,0,2:T(8,128)S(1)} %copy.35, s32[1024]{0:T(1024)S(1)} %pad_clamp_fusion), kind=kCustom, calls=%fused_computation.3.clone | custom fusion | bytes 2624000 | tf_op jit(solution)/shard_map/jit(_take)/gather | solution.py:31
  85.1 3.4 %gather_fusion.2 = f32[640,8,64]{2,1,0:T(8,128)} fusion(f32[8,64,256]{1,0,2:T(8,128)S(1)} %copy.34, s32[1024]{0:T(1024)S(1)} %pad_clamp_fusion), kind=kCustom, calls=%fused_computation.1.clone | custom fusion | bytes 2624000 | tf_op jit(solution)/shard_map/jit(_take)/gather | solution.py:30
  88.5 9.0 %fusion.2 = (f32[640,8]{1,0:T(8,128)S(1)}, f32[640,8]{1,0:T(8,128)S(1)}, f32[640,8]{1,0:T(8,128)S(1)}, f32[640,8]{1,0:T(8,128)S(1)}) fusion(f32[640,8,64]{2,1,0:T(8,128)} %gather_fusion.2, f32[640,64]{1,0:T(8,128)S(1)} %copy.77, pred[640]{0:T(1024)(128)(4,1)S(1)} %get-tuple-element.13, f32[640,64]{1,0:T(8,128)} %copy.78, f32[640,8,64]{2,1,0:T(8,128)} %gather_fusion.3), kind=kLoop, calls=%fused_computation.10 | loop fusion | flops 3256320 | bytes 3031680
  98.1 76.1 %all_gather.3 = bf16[2,256,640]{2,0,1:T(2,128)(2,1)S(1)} all-gather(bf16[2,8,640]{2,0,1:T(2,128)(2,1)S(1)} %copy.36), channel_id=1, replica_groups=mesh['tr'=8,'tc'=4,'ga'=16] {'tr','tc'}, dimensions={1}, use_global_device_ids=true | all-gather | bytes 675840 | tf_op jit(solution)/shard_map/all_gather | solution.py:75
  177.1 89.9 %reduce-scatter.4.cloned.1.call-done = f32[16,16]{1,0:T(8,128)} async-done(((f32[256,16]{1,0:T(8,128)}), f32[16,16]{1,0:T(8,128)}) %reduce-scatter.4.cloned.1.call-update) | async-done | bytes 1040
  (49 shorter events, 18.6 us)
Async XLA Ops:
  6.5 3.6 %copy-start = (bf16[2,16,4,4096]{3,2,1,0:T(4,128)(2,1)S(1)}, bf16[2,16,4,4096]{3,2,1,0:T(4,128)(2,1)}, u32[]{:S(2)}) copy-start(bf16[2,16,4,4096]{3,2,1,0:T(4,128)(2,1)} %param.12) | copy-start | bytes 3145732
  19.3 1.2 copy-start.1
  29.3 20.6 %copy-start.2 = (f32[640]{0:T(1024)S(1)}, f32[640]{0:T(1024)}, u32[]{:S(2)}) copy-start(f32[640]{0:T(1024)} %param.17) | copy-start | bytes 7684
  32.2 34.1 %all-to-all-start = ((f32[16,1,16384]{2,1,0:T(1,128)}), f32[16,1,16384]{2,1,0:T(1,128)S(1)}, u32[]{:S(2)}, u32[]{:S(2)}) async-start(f32[16,1,16384]{2,1,0:T(1,128)} %reshape.95), calls=%async_computation | async-start | bytes 2097152 | tf_op jit(solution)/shard_map/all_to_all | solution.py:62
  46.5 220.5 %reduce-scatter.4.cloned.1.call-start = ((), (), s32[]{:S(2)}) async-start(), calls=%async_computation.2 | async-start | bytes 139264
Sparse Core Ops, SparseCore 0:
  177.2 89.6 reduce-scatter.3
where the time goes:
time: 277 us; the launch traced here: 275 us
  waiting for transfers between devices  106 us (38%)
  blocking collectives  76.1 us (27%)
  local copies, waits for them, and re-layouts  32.5 us (12%)
  other arithmetic  21.2 us (8%)
  starting transfers between devices  14.3 us (5%)
  between operations  13.6 us (5%)
  matrix products  11.1 us (4%)
    unnamed x2, waiting for transfers between devices  89.9 us
    all_gather x1, blocking collectives, body(): piece = lax.all_gather(weighted, ('tr', 'tc'), axis=1, tiled=True)  76.1 us
    all_to_all x1, waiting for transfers between devices, body(): lax.all_to_all(stacked, 'ga', split_axis=3, concat_axis=2, tiled=True)  16.5 us
    all_to_all x1, starting transfers between devices, body(): lax.all_to_all(stacked, 'ga', split_axis=3, concat_axis=2, tiled=True)  14.3 us
    unnamed x2, other arithmetic  9.64 us
    unnamed x14, local copies, waits for them, and re-layouts  9.25 us
  transfers between devices with their start and end apart: 2, of which 2 were waited for; matrix products, arithmetic and copies ran while one was open for 1% of the time, Pallas kernels for 0%

commit v1 on v0

v1 whole, which is shorter than its diff:
```python
import functools
import math

import jax
import jax.numpy as jnp
import numpy as np
from jax import lax
from jax.experimental import pallas as pl
from jax.experimental.pallas import tpu as pltpu
from jax.sharding import PartitionSpec as P

LANES = 128
COUNT = 8
SLAB = 4


def halves(array):
    high = array.astype(jnp.bfloat16)
    low = (array - high.astype(jnp.float32)).astype(jnp.bfloat16)
    return high, low


def tables(points):
    indices = np.arange(points)
    angles = 2.0 * np.pi * (np.outer(indices, indices) % points) / points
    pair = np.eye(2)
    along_z = np.concatenate([np.kron(pair, np.cos(angles)), np.kron(pair, np.sin(angles))], axis=1)
    half = points // 2
    short = np.arange(half)
    angles = 2.0 * np.pi * (np.outer(short, short) % half) / half
    planes = np.eye(SLAB)
    cosine, sine = np.kron(np.cos(angles), planes), np.kron(np.sin(angles), planes)
    along_y = np.block([[cosine, sine], [-sine, cosine]])
    turn = 2.0 * np.pi * np.repeat(short, SLAB) / points
    ones = np.ones((half * SLAB, points))
    twist = np.stack(
        [
            np.concatenate([ones, ones * np.cos(turn)[:, None]], axis=1),
            np.concatenate([0.0 * ones, ones * -np.sin(turn)[:, None]], axis=1),
        ]
    )

    return tuple(table.astype(np.float32) for table in (along_z, along_y, twist))


def unit_circle(steps, points):
    quarter = points // 4
    shifted = steps + quarter // 2
    turn = (shifted // quarter) & 3
    angle = ((shifted & (quarter - 1)) - quarter // 2).astype(jnp.float32) * (2.0 * math.pi / points)
    square = angle * angle
    sine = angle * (
        1.0 + square * (-1 / 6 + square * (1 / 120 + square * (-1 / 5040 + square * (1 / 362880))))
    )
    cosine = 1.0 + square * (
        -1 / 2
        + square * (1 / 24 + square * (-1 / 720 + square * (1 / 40320 - square * (1 / 3628800))))
    )
    odd = (turn & 1) == 1
    first = jnp.where(odd, sine, cosine)
    second = jnp.where(odd, cosine, sine)
    return (
        jnp.where((turn == 1) | (turn == 2), -first, first),
        jnp.where(turn >= 2, -second, second),
    )


def transform_kernel(
    points,
    valence_ids,
    conduct_ids,
    position,
    valence,
    conduction,
    envelope,
    grid,
    along_z,
    along_y,
    twist,
    out,
    field,
    waves,
):
    rows = points // 2 * SLAB
    tiles = grid.shape[0] // out.shape[0]
    blocks = out.shape[0]
    dot = functools.partial(jnp.dot, preferred_element_type=jnp.float32)

    wave_x = grid[...] // (points * points)
    for plane in range(SLAB):
        steps = ((position[0] * SLAB + plane) * wave_x) & (points - 1)
        cosine, sine = unit_circle(steps, points)
        waves[2 * plane] = cosine
        waves[2 * plane + 1] = sine

    z_high, z_low = halves(along_z[...])
    y_high, y_low = halves(along_y[...])

    common_real = envelope[0].astype(jnp.float32)
    common_imag = envelope[1].astype(jnp.float32)
    lane = lax.broadcasted_iota(jnp.int32, (rows, LANES), 1)
    sign = jnp.where(lane < points, 1.0, -1.0).astype(jnp.float32)
    for first in range(0, COUNT, 2):
        parts = []
        for t in (first, first + 1):
            v, c = valence_ids[t], conduct_ids[t]
            left_real = valence[0, v].astype(jnp.float32)
            left_imag = valence[1, v].astype(jnp.float32)
            right_real = conduction[0, c].astype(jnp.float32) + common_real
            right_imag = conduction[1, c].astype(jnp.float32) + common_imag
            parts.append(left_real * right_real + left_imag * right_imag)
            parts.append(left_real * right_imag - left_imag * right_real)
        high, low = halves(jnp.concatenate(parts, axis=0))
        moved = dot(high, z_high) + (dot(low, z_high) + dot(high, z_low))
        columns = []
        for t in range(2):
            real = moved[2 * t * rows : (2 * t + 1) * rows]
            imag = moved[(2 * t + 1) * rows : (2 * t + 2) * rows]
            columns.append(
                jnp.concatenate(
                    [real[:, :LANES] + imag[:, LANES:], imag[:, :LANES] - real[:, LANES:]], axis=0
                )
            )
        high, low = halves(jnp.concatenate(columns, axis=1))
        moved = dot(y_high, high) + (dot(y_high, low) + dot(y_low, high))
        for t in range(2):
            real = moved[:rows, t * LANES : (t + 1) * LANES]
            imag = moved[rows:, t * LANES : (t + 1) * LANES]
            turned_real = real * twist[0] - imag * twist[1]
            turned_imag = real * twist[1] + imag * twist[0]
            start = (first + t) * rows
            field[0, start : start + rows] = pltpu.roll(turned_real, points, 1) + sign * turned_real
            field[1, start : start + rows] = pltpu.roll(turned_imag, points, 1) + sign * turned_imag

    half = blocks // 2

    def one_pair(k, carry):
        picked = []
        for part in range(2):
            for y in range(SLAB):
                for x in range(SLAB):
                    start = (k * SLAB + y) * SLAB + x
                    picked.append(field[part, pl.ds(start, COUNT, stride=rows), :])
        high, low = halves(jnp.concatenate(picked, axis=0))
        source = jnp.concatenate([high, low], axis=1)
        chosen = []
        for side in range(2):
            row = (k + half * side) * tiles
            index = [grid[pl.ds(row + j, 1), :] for j in range(tiles)]
            depth = lax.broadcasted_iota(jnp.int32, (points, LANES), 0)
            match = jnp.concatenate(
                [jnp.where((i & (points - 1)) == depth, 1.0, 0.0) for i in index], axis=1
            ).astype(jnp.bfloat16)
            empty = jnp.zeros_like(match)
            order = [match, empty] if side == 0 else [empty, match]
            chosen.append(jnp.concatenate(order + order, axis=0))
        values = dot(source, jnp.concatenate(chosen, axis=1))
        for side in range(2):
            block = k + half * side
            for j in range(tiles):
                row = block * tiles + j
                at = (side * tiles + j) * LANES
                index = jnp.broadcast_to(grid[pl.ds(row, 1), :], (COUNT, LANES))
                wave_y = (index // points) & (SLAB - 1)
                total_real = jnp.zeros((COUNT, LANES), jnp.float32)
                total_imag = jnp.zeros((COUNT, LANES), jnp.float32)
                for x in range(SLAB):
                    pieces = []
                    for part in range(2):
                        of = [
                            values[((part * SLAB + y) * SLAB + x) * COUNT :][:COUNT, at : at + LANES]
                            for y in range(SLAB)
                        ]
                        pieces.append(
                            jnp.where(
                                wave_y < 2,
                                jnp.where(wave_y == 0, of[0], of[1]),
                                jnp.where(wave_y == 2, of[2], of[3]),
                            )
                        )
                    cosine = waves[2 * x, pl.ds(row, 1), :]
                    sine = waves[2 * x + 1, pl.ds(row, 1), :]
                    total_real += pieces[0] * cosine + pieces[1] * sine
                    total_imag += pieces[1] * cosine - pieces[0] * sine
                out[block, j * 2 * COUNT : (j * 2 + 1) * COUNT] = total_real.astype(out.dtype)
                out[block, (j * 2 + 1) * COUNT : (j * 2 + 2) * COUNT] = total_imag.astype(out.dtype)
        return carry

    lax.fori_loop(0, half, one_pair, 0)


def weight_kernel(scale, partial, coulomb, out):
    total = partial[0].astype(jnp.float32)
    for source in range(1, partial.shape[0]):
        total += partial[source].astype(jnp.float32)
    root = jnp.sqrt(coulomb[...])
    height = 2 * COUNT
    pieces = []
    for j in range(total.shape[0] // height):
        factor = root[:, j * LANES : (j + 1) * LANES]
        pieces.append((total[j * height : (j + 1) * height] * scale) * factor)
    weighted = jnp.concatenate(pieces, axis=0).astype(jnp.bfloat16)
    for target in range(out.shape[0]):
        out[target] = weighted


def panel_kernel(own, gathered, out):
    senders, height = gathered.shape[0], 2 * COUNT
    tiles = gathered.shape[1] // height
    first, second, right = [], [], []
    for j in range(tiles):
        left = own[0, j * height : (j + 1) * height].astype(jnp.float32)
        real, imag = left[:COUNT], left[COUNT:]
        empty = jnp.zeros((LANES - height, LANES), jnp.float32)
        first.append(jnp.concatenate([real, -imag, empty], axis=0).astype(jnp.bfloat16))
        second.append(jnp.concatenate([imag, real, empty], axis=0).astype(jnp.bfloat16))
        right.append(gathered[:, j * height : (j + 1) * height].reshape(senders * height, LANES))
    right = jnp.concatenate(right, axis=1)
    contract = (((1,), (1,)), ((), ()))

    def product(left):
        result = lax.dot_general(
            right, jnp.concatenate(left, axis=1), contract, preferred_element_type=jnp.float32
        )
        return result.reshape(senders, 2, COUNT, LANES)

    total = product(first)[:, 0] + product(second)[:, 1]
    out[...] = total.reshape(out.shape)


def sum_kernel(scale, partial, out):
    total = partial[0]
    for source in range(1, partial.shape[0]):
        total += partial[source]
    turned = (total * scale).T[: 2 * COUNT]
    out[...] = turned[:, : out.shape[2]].reshape(out.shape)


def body(valence, conduction, envelope, valence_index, conduction_index, grid_index, coulomb):
    points = math.isqrt(valence.shape[-1])
    groups = lax.axis_size("ga")
    senders = lax.axis_size("tr") * lax.axis_size("tc")
    per_device = coulomb.shape[0]
    tiles = per_device // LANES
    rows = points // 2 * SLAB
    transitions = senders * COUNT

    def turned(array):
        lead = array.shape[:-2]
        split = array.reshape(lead + (SLAB, points // 2, LANES))
        return jnp.swapaxes(split, -3, -2).reshape(lead + (rows, LANES))

    along_z, along_y, twist = tables(points)
    position = lax.axis_index("ga").astype(jnp.int32).reshape(1)
    smem = pl.BlockSpec(memory_space=pltpu.SMEM)
    vmem = pl.BlockSpec(memory_space=pltpu.VMEM)
    limit = pltpu.CompilerParams(vmem_limit_bytes=40 * 1024 * 1024)
    partial = pl.pallas_call(
        functools.partial(transform_kernel, points),
        out_shape=jax.ShapeDtypeStruct((groups, tiles * 2 * COUNT, LANES), jnp.float32),
        in_specs=[smem] * 3 + [vmem] * 7,
        out_specs=vmem,
        scratch_shapes=[
            pltpu.VMEM((2, COUNT * rows, LANES), jnp.float32),
            pltpu.VMEM((2 * SLAB, groups * tiles, LANES), jnp.float32),
        ],
        compiler_params=limit,
        name="transform",
    )(
        valence_index,
        conduction_index,
        position,
        turned(valence),
        turned(conduction),
        turned(envelope),
        grid_index.reshape(groups * tiles, LANES),
        along_z,
        along_y,
        twist,
    )
    partial = lax.all_to_all(partial, "ga", split_axis=0, concat_axis=0, tiled=True)
    copies = pl.pallas_call(
        functools.partial(weight_kernel, float(points) ** -1.5),
        out_shape=jax.ShapeDtypeStruct((senders, tiles * 2 * COUNT, LANES), jnp.bfloat16),
        in_specs=[vmem] * 2,
        out_specs=vmem,
        compiler_params=limit,
        name="weight",
    )(partial, coulomb.reshape(1, per_device))
    gathered = lax.all_to_all(copies, ("tr", "tc"), split_axis=0, concat_axis=0, tiled=True)
    width = transitions // groups
    terms = pl.pallas_call(
        panel_kernel,
        out_shape=jax.ShapeDtypeStruct((groups, width, LANES), jnp.float32),
        in_specs=[vmem] * 2,
        out_specs=vmem,
        compiler_params=limit,
        name="panel",
    )(copies, gathered)
    terms = lax.all_to_all(terms, "ga", split_axis=0, concat_axis=0, tiled=True)
    return pl.pallas_call(
        functools.partial(sum_kernel, 1.0 / (per_device * groups)),
        out_shape=jax.ShapeDtypeStruct((2, COUNT, width), jnp.float32),
        in_specs=[vmem],
        out_specs=vmem,
        compiler_params=limit,
        name="total",
    )(terms)


def solution(mesh):
    placed = (
        P(None, None, "ga", None),
        P(None, None, "ga", None),
        P(None, "ga", None),
        P(("tr", "tc")),
        P(("tr", "tc")),
        P(),
        P("ga"),
    )
    return jax.shard_map(
        body, mesh=mesh, in_specs=placed, out_specs=P(None, ("tr", "tc"), "ga"), check_vma=False
    )
```

time: 277 us -> 97.7 us (0.35)
  waiting for transfers between devices: 106 us -> 15.6 us
  blocking collectives: 76.1 us -> 50.5 us
  local copies, waits for them, and re-layouts: 32.5 us -> 7.5 us
  other arithmetic: 21.2 us -> 0 us
  between operations: 13.6 us -> 0.04 us
  matrix products: 11.1 us -> 0 us
  Pallas kernels: 0 us -> 9.13 us
    unnamed x2 -> x0, waiting for transfers between devices: 89.9 us -> none
    all_gather x1 -> x0, blocking collectives: 76.1 us -> none  [body(): piece = lax.all_gather(weighted, ('tr', 'tc'), axis=1, tiled=True)]
    all_to_all x0 -> x2, blocking collectives: none -> 50.5 us  [the longest x1 35.3 us: body(): lax.all_to_all(copies, ('tr', 'tc'), split_axis=0, concat_axis=0, tiled=T...]
    dot_general x12 -> x0, matrix products: 11.1 us -> none  [the longest x2 3.27 us: section(): jnp.einsum(form, real_part, cosine, precision=precise)]
    gather x4 -> x0, local copies, waits for them, and re-layouts: 10.2 us -> none  [the longest x1 3.63 us: plane_sum(): picked_imag = jnp.take(data_imag, columns, axis=2)]
    unnamed x2 -> x0, other arithmetic: 9.64 us -> none
    pallas_call x0 -> x4, Pallas kernels: none -> 9.13 us  [the longest x1 7.91 us: body(): pl.pallas_call(functools.partial(transform_kernel, points), out_shape=jax...]
    squeeze x4 -> x0, local copies, waits for them, and re-layouts: 5.75 us -> none  [the longest x2 2.87 us: body(): flat[1]]
  transfers between devices with their start and end apart: 2 -> 1, of which waited for: 2 -> 1; matrix products, arithmetic and copies ran while one was open for 1% -> 0% of each run, Pallas kernels for 0% -> 0%
where the time goes in v1:
time: 97.7 us; the launch traced here: 97.2 us
  blocking collectives  50.5 us (52%)
  waiting for transfers between devices  15.6 us (16%)
  starting transfers between devices  14.4 us (15%)
  Pallas kernels  9.13 us (9%)
  local copies, waits for them, and re-layouts  7.5 us (8%)
    all_to_all x1, blocking collectives, body(): lax.all_to_all(copies, ('tr', 'tc'), split_axis=0, concat_axis=0, tiled=T...  35.3 us
    all_to_all x1, waiting for transfers between devices, body(): lax.all_to_all(partial, 'ga', split_axis=0, concat_axis=0, tiled=True)  15.6 us
    all_to_all x1, blocking collectives, body(): terms = lax.all_to_all(terms, 'ga', split_axis=0, concat_axis=0, tiled=True)  15.2 us
    all_to_all x1, starting transfers between devices, body(): lax.all_to_all(partial, 'ga', split_axis=0, concat_axis=0, tiled=True)  14.4 us
    pallas_call x1, Pallas kernels, body(): pl.pallas_call(functools.partial(transform_kernel, points), out_shape=jax...  7.91 us
    unnamed x20, local copies, waits for them, and re-layouts  7.5 us
  transfers between devices with their start and end apart: 1, of which 1 were waited for; matrix products, arithmetic and copies ran while one was open for 0% of the time, Pallas kernels for 0%

profile of v1, /device:TPU:1, one launch (start us, length us, event | category | flops | bytes accessed | tf_op | source)
XLA Modules:
  0.0 97.2 jit_solution(18182375161763137024)
XLA Ops:
  0.0 0.0 copy-start.7
  0.0 0.0 copy-start.8
  0.0 0.7 copy-done.7
  0.7 0.0 copy-done.8
  0.7 0.0 copy-start
  0.7 1.2 %copy-done = bf16[2,16,4,4096]{3,2,1,0:T(4,128)(2,1)S(1)} copy-done((bf16[2,16,4,4096]{3,2,1,0:T(4,128)(2,1)S(1)}, bf16[2,16,4,4096]{3,2,1,0:T(4,128)(2,1)}, u32[]{:S(2)}) %copy-start) | copy-done | bytes 1048600
  1.9 0.0 copy-start.1
  1.9 1.2 %copy-done.1 = bf16[2,16,4,4096]{3,2,1,0:T(4,128)(2,1)S(1)} copy-done((bf16[2,16,4,4096]{3,2,1,0:T(4,128)(2,1)S(1)}, bf16[2,16,4,4096]{3,2,1,0:T(4,128)(2,1)}, u32[]{:S(2)}) %copy-start.1) | copy-done | bytes 1048600
  3.1 0.0 copy-start.2
  3.1 0.9 copy-done.2
  4.1 0.0 copy-start.3
  4.1 0.9 copy-done.3
  5.0 0.9 copy-done.4
  5.9 0.8 copy-done.5
  6.7 0.8 copy-done.6
  7.5 7.9 %transform.1 = f32[16,80,128]{2,1,0:T(8,128)} custom-call(s32[8]{0:T(128)S(1)} %copy-done.7, s32[8]{0:T(128)S(1)} %copy-done.8, s32[1]{0:T(128)} %bitcast.position, bf16[2,16,128,128]{3,2,1,0:T(8,128)(2,1)S(1)} %bitcast.17, bf16[2,16,128,128]{3,2,1,0:T(8,128)(2,1)S(1)} %bitcast.18, bf16[2,128,128]{2,1,0:T(8,128)(2,1)S(1)} %bitcast.19, ...), custom_call_target="tpu_custom_call" | custom-call | tf_op jit(solution)/shard_map/transform/pallas_call | solution.py:258
  15.4 14.4 %all-to-all-start = ((f32[16,80,128]{2,1,0:T(8,128)}), f32[16,80,128]{2,1,0:T(8,128)S(1)}, u32[]{:S(2)}, u32[]{:S(2)}) async-start(f32[16,80,128]{2,1,0:T(8,128)} %transform.1), calls=%async_computation | async-start | bytes 1310720 | tf_op jit(solution)/shard_map/all_to_all | solution.py:281
  29.8 0.0 copy-done.9
  29.8 15.6 %all-to-all-done.partial = f32[16,80,128]{2,1,0:T(8,128)S(1)} async-done(((f32[16,80,128]{2,1,0:T(8,128)}), f32[16,80,128]{2,1,0:T(8,128)S(1)}, u32[]{:S(2)}, u32[]{:S(2)}) %all-to-all-start) | async-done | bytes 655392 | tf_op jit(solution)/shard_map/all_to_all | solution.py:281
  45.4 0.1 weight.1.own
  45.5 35.3 %all_to_all.15.gathered = bf16[32,80,128]{2,1,0:T(8,128)(2,1)S(1)} all-to-all(bf16[32,80,128]{2,1,0:T(8,128)(2,1)S(1)} %weight.1.own), channel_id=1, replica_groups=mesh['tr'=8,'tc'=4,'ga'=16] {'tr','tc'}, dimensions={0} | all-to-all | bytes 1310720 | tf_op jit(solution)/shard_map/all_to_all | solution.py:290
  80.8 0.5 panel.1
  81.3 15.2 %all_to_all.16.partial = f32[16,16,128]{2,1,0:T(8,128)S(1)} all-to-all(f32[16,16,128]{2,1,0:T(8,128)S(1)} %panel.1), channel_id=1, replica_groups=mesh['tr'=8,'tc'=4,'ga'=16] {'ga'}, dimensions={0} | all-to-all | bytes 262144 | tf_op jit(solution)/shard_map/all_to_all | solution.py:300
  96.5 0.7 total.1
  (5 shorter events, 0.0 us)
Async XLA Ops:
  0.0 0.7 copy-start.7
  0.0 0.7 copy-start.8
  0.7 1.2 %copy-start = (bf16[2,16,4,4096]{3,2,1,0:T(4,128)(2,1)S(1)}, bf16[2,16,4,4096]{3,2,1,0:T(4,128)(2,1)}, u32[]{:S(2)}) copy-start(bf16[2,16,4,4096]{3,2,1,0:T(4,128)(2,1)} %param.10) | copy-start | bytes 3145732
  1.9 1.2 %copy-start.1 = (bf16[2,16,4,4096]{3,2,1,0:T(4,128)(2,1)S(1)}, bf16[2,16,4,4096]{3,2,1,0:T(4,128)(2,1)}, u32[]{:S(2)}) copy-start(bf16[2,16,4,4096]{3,2,1,0:T(4,128)(2,1)} %param.11) | copy-start | bytes 3145732
  3.1 0.9 copy-start.2
  4.1 0.9 copy-start.3
  5.0 0.9 copy-start.4
  5.9 0.8 copy-start.5
  6.7 0.8 copy-start.6
  15.4 14.4 %copy-start.9 = (f32[640]{0:T(1024)S(1)}, f32[640]{0:T(1024)}, u32[]{:S(2)}) copy-start(f32[640]{0:T(1024)} %param.16) | copy-start | bytes 7684
  15.4 30.0 %all-to-all-start = ((f32[16,80,128]{2,1,0:T(8,128)}), f32[16,80,128]{2,1,0:T(8,128)S(1)}, u32[]{:S(2)}, u32[]{:S(2)}) async-start(f32[16,80,128]{2,1,0:T(8,128)} %transform.1), calls=%async_computation | async-start | bytes 1310720 | tf_op jit(solution)/shard_map/all_to_all | solution.py:281

commit v2 on v1

--- a/solution.py
+++ b/solution.py
@@ -73,18 +73,54 @@
     valence,
     conduction,
     envelope,
+    grid_source,
+    along_z_source,
+    along_y_source,
+    twist_source,
+    out,
+    left_rows,
+    right_rows,
+    common,
     grid,
     along_z,
     along_y,
     twist,
-    out,
     field,
     waves,
+    arrived,
 ):
     rows = points // 2 * SLAB
     tiles = grid.shape[0] // out.shape[0]
     blocks = out.shape[0]
     dot = functools.partial(jnp.dot, preferred_element_type=jnp.float32)
+
+    copies = []
+
+    def fetch(source, target):
+        copy = pltpu.make_async_copy(source, target, arrived.at[len(copies)])
+        copy.start()
+        copies.append(copy)
+        return copy
+
+    whole = [
+        fetch(source, target)
+        for source, target in (
+            (grid_source, grid),
+            (along_z_source, along_z),
+            (envelope, common),
+            (along_y_source, along_y),
+            (twist_source, twist),
+        )
+    ]
+    bands = []
+    for t in range(COUNT):
+        bands.append(
+            (
+                fetch(valence.at[:, valence_ids[t]], left_rows.at[t]),
+                fetch(conduction.at[:, conduct_ids[t]], right_rows.at[t]),
+            )
+        )
+    whole[0].wait()
 
     wave_x = grid[...] // (points * points)
     for plane in range(SLAB):
@@ -93,21 +129,24 @@
         waves[2 * plane] = cosine
         waves[2 * plane + 1] = sine
 
+    for copy in whole[1:]:
+        copy.wait()
     z_high, z_low = halves(along_z[...])
     y_high, y_low = halves(along_y[...])
 
-    common_real = envelope[0].astype(jnp.float32)
-    common_imag = envelope[1].astype(jnp.float32)
+    common_real = common[0].astype(jnp.float32)
+    common_imag = common[1].astype(jnp.float32)
     lane = lax.broadcasted_iota(jnp.int32, (rows, LANES), 1)
     sign = jnp.where(lane < points, 1.0, -1.0).astype(jnp.float32)
     for first in range(0, COUNT, 2):
         parts = []
         for t in (first, first + 1):
-            v, c = valence_ids[t], conduct_ids[t]
-            left_real = valence[0, v].astype(jnp.float32)
-            left_imag = valence[1, v].astype(jnp.float32)
-            right_real = conduction[0, c].astype(jnp.float32) + common_real
-            right_imag = conduction[1, c].astype(jnp.float32) + common_imag
+            for copy in bands[t]:
+                copy.wait()
+            left_real = left_rows[t, 0].astype(jnp.float32)
+            left_imag = left_rows[t, 1].astype(jnp.float32)
+            right_real = right_rows[t, 0].astype(jnp.float32) + common_real
+            right_imag = right_rows[t, 1].astype(jnp.float32) + common_imag
             parts.append(left_real * right_real + left_imag * right_imag)
             parts.append(left_real * right_imag - left_imag * right_real)
         high, low = halves(jnp.concatenate(parts, axis=0))
@@ -199,17 +238,29 @@
     for j in range(total.shape[0] // height):
         factor = root[:, j * LANES : (j + 1) * LANES]
         pieces.append((total[j * height : (j + 1) * height] * scale) * factor)
-    weighted = jnp.concatenate(pieces, axis=0).astype(jnp.bfloat16)
-    for target in range(out.shape[0]):
-        out[target] = weighted
-
-
-def panel_kernel(own, gathered, out):
-    senders, height = gathered.shape[0], 2 * COUNT
+    out[...] = jnp.concatenate(pieces, axis=0).astype(jnp.bfloat16)
+
+
+def stack_kernel(position, *refs):
+    pieces, out = refs[:-1], refs[-1]
+    for shift, piece in enumerate(pieces):
+        out[(position[0] - shift + len(pieces)) % len(pieces)] = piece[...]
+
+
+def panel_kernel(place, own, *refs):
+    tcs = place[1]
+    chips = lax.axis_size("tc")
+    stacks, outs, (gathered, terms) = refs[:chips], refs[chips:-2], refs[-2:]
+    lines = stacks[0].shape[0]
+    for shift, stack in enumerate(stacks):
+        line = (tcs - shift + chips) % chips
+        for other in range(lines):
+            gathered[other * chips + line] = stack[other]
+    senders, height = lines * chips, 2 * COUNT
     tiles = gathered.shape[1] // height
     first, second, right = [], [], []
     for j in range(tiles):
-        left = own[0, j * height : (j + 1) * height].astype(jnp.float32)
+        left = own[j * height : (j + 1) * height].astype(jnp.float32)
         real, imag = left[:COUNT], left[COUNT:]
         empty = jnp.zeros((LANES - height, LANES), jnp.float32)
         first.append(jnp.concatenate([real, -imag, empty], axis=0).astype(jnp.bfloat16))
@@ -225,46 +276,60 @@
         return result.reshape(senders, 2, COUNT, LANES)
 
     total = product(first)[:, 0] + product(second)[:, 1]
-    out[...] = total.reshape(out.shape)
-
-
-def sum_kernel(scale, partial, out):
-    total = partial[0]
-    for source in range(1, partial.shape[0]):
-        total += partial[source]
+    terms[...] = total.reshape(terms.shape)
+    for partner, out in enumerate(outs):
+        out[...] = terms[place[0] ^ partner]
+
+
+def sum_kernel(scale, *refs):
+    out = refs[-1]
+    total = refs[0][...]
+    for piece in refs[1:-1]:
+        total += piece[...]
     turned = (total * scale).T[: 2 * COUNT]
     out[...] = turned[:, : out.shape[2]].reshape(out.shape)
 
 
 def body(valence, conduction, envelope, valence_index, conduction_index, grid_index, coulomb):
     points = math.isqrt(valence.shape[-1])
-    groups = lax.axis_size("ga")
-    senders = lax.axis_size("tr") * lax.axis_size("tc")
+    groups, lines, chips = (lax.axis_size(name) for name in ("ga", "tr", "tc"))
     per_device = coulomb.shape[0]
     tiles = per_device // LANES
     rows = points // 2 * SLAB
-    transitions = senders * COUNT
+    height = tiles * 2 * COUNT
+    width = lines * chips * COUNT // groups
 
     def turned(array):
         lead = array.shape[:-2]
         split = array.reshape(lead + (SLAB, points // 2, LANES))
         return jnp.swapaxes(split, -3, -2).reshape(lead + (rows, LANES))
 
-    along_z, along_y, twist = tables(points)
-    position = lax.axis_index("ga").astype(jnp.int32).reshape(1)
+    position, line, chip = (
+        lax.axis_index(name).astype(jnp.int32).reshape(1) for name in ("ga", "tr", "tc")
+    )
     smem = pl.BlockSpec(memory_space=pltpu.SMEM)
     vmem = pl.BlockSpec(memory_space=pltpu.VMEM)
-    limit = pltpu.CompilerParams(vmem_limit_bytes=40 * 1024 * 1024)
+    anywhere = pl.BlockSpec(memory_space=pl.ANY)
+    limit = pltpu.CompilerParams(vmem_limit_bytes=16 * 1024 * 1024)
+    along_z, along_y, twist = tables(points)
     partial = pl.pallas_call(
         functools.partial(transform_kernel, points),
-        out_shape=jax.ShapeDtypeStruct((groups, tiles * 2 * COUNT, LANES), jnp.float32),
-        in_specs=[smem] * 3 + [vmem] * 7,
+        out_shape=jax.ShapeDtypeStruct((groups, height, LANES), jnp.float32),
+        in_specs=[smem] * 3 + [anywhere] * 7,
         out_specs=vmem,
         scratch_shapes=[
+            pltpu.VMEM((COUNT, 2, rows, LANES), jnp.bfloat16),
+            pltpu.VMEM((COUNT, 2, rows, LANES), jnp.bfloat16),
+            pltpu.VMEM((2, rows, LANES), jnp.bfloat16),
+            pltpu.VMEM((groups * tiles, LANES), jnp.int32),
+            pltpu.VMEM(along_z.shape, jnp.float32),
+            pltpu.VMEM(along_y.shape, jnp.float32),
+            pltpu.VMEM(twist.shape, jnp.float32),
             pltpu.VMEM((2, COUNT * rows, LANES), jnp.float32),
             pltpu.VMEM((2 * SLAB, groups * tiles, LANES), jnp.float32),
+            pltpu.SemaphoreType.DMA((5 + 2 * COUNT,)),
         ],
-        compiler_params=limit,
+        compiler_params=pltpu.CompilerParams(vmem_limit_bytes=62 * 1024 * 1024),
         name="transform",
     )(
         valence_index,
@@ -279,33 +344,53 @@
         twist,
     )
     partial = lax.all_to_all(partial, "ga", split_axis=0, concat_axis=0, tiled=True)
-    copies = pl.pallas_call(
+    own = pl.pallas_call(
         functools.partial(weight_kernel, float(points) ** -1.5),
-        out_shape=jax.ShapeDtypeStruct((senders, tiles * 2 * COUNT, LANES), jnp.bfloat16),
+        out_shape=jax.ShapeDtypeStruct((height, LANES), jnp.bfloat16),
         in_specs=[vmem] * 2,
         out_specs=vmem,
         compiler_params=limit,
         name="weight",
     )(partial, coulomb.reshape(1, per_device))
-    gathered = lax.all_to_all(copies, ("tr", "tc"), split_axis=0, concat_axis=0, tiled=True)
-    width = transitions // groups
+
+    def shifted(array, name, shift):
+        size = lax.axis_size(name)
+        return lax.ppermute(array, name, [(i, (i + shift) % size) for i in range(size)])
+
+    pieces = [own] + [shifted(own, "tr", shift) for shift in range(1, lines)]
+    stack = pl.pallas_call(
+        stack_kernel,
+        out_shape=jax.ShapeDtypeStruct((lines, height, LANES), jnp.bfloat16),
+        in_specs=[smem] + [vmem] * lines,
+        out_specs=vmem,
+        compiler_params=limit,
+        name="stack",
+    )(line, *pieces)
+    stacks = [stack] + [shifted(stack, "tc", shift) for shift in range(1, chips)]
     terms = pl.pallas_call(
         panel_kernel,
-        out_shape=jax.ShapeDtypeStruct((groups, width, LANES), jnp.float32),
-        in_specs=[vmem] * 2,
-        out_specs=vmem,
+        out_shape=[jax.ShapeDtypeStruct((width, LANES), jnp.float32)] * groups,
+        in_specs=[smem] + [vmem] * (1 + chips),
+        out_specs=[vmem] * groups,
+        scratch_shapes=[
+            pltpu.VMEM((lines * chips, height, LANES), jnp.bfloat16),
+            pltpu.VMEM((groups, width, LANES), jnp.float32),
+        ],
         compiler_params=limit,
         name="panel",
-    )(copies, gathered)
-    terms = lax.all_to_all(terms, "ga", split_axis=0, concat_axis=0, tiled=True)
+    )(jnp.concatenate([position, chip]), own, *stacks)
+    pieces = [terms[0]] + [
+        lax.ppermute(terms[partner], "ga", [(i, i ^ partner) for i in range(groups)])
+        for partner in range(1, groups)
+    ]
     return pl.pallas_call(
         functools.partial(sum_kernel, 1.0 / (per_device * groups)),
         out_shape=jax.ShapeDtypeStruct((2, COUNT, width), jnp.float32),
-        in_specs=[vmem],
+        in_specs=[vmem] * groups,
         out_specs=vmem,
         compiler_params=limit,
         name="total",
-    )(terms)
+    )(*pieces)
 
 
 def solution(mesh):

time: 97.7 us -> 164 us (1.68)
  starting transfers between devices: 14.4 us -> 129 us
  blocking collectives: 50.5 us -> 0 us
  local copies, waits for them, and re-layouts: 7.5 us -> 0.01 us
  waiting for transfers between devices: 15.6 us -> 22.2 us
  Pallas kernels: 9.13 us -> 11.7 us
    ppermute x0 -> x25, starting transfers between devices: none -> 115 us  [the longest x15 68.8 us: body(): lax.ppermute(terms[partner], 'ga', [(i, i ^ partner) for i in range(group...]
    all_to_all x2 -> x0, blocking collectives: 50.5 us -> none  [the longest x1 35.3 us: body(): lax.all_to_all(copies, ('tr', 'tc'), split_axis=0, concat_axis=0, tiled=T...]
    unnamed x20 -> x2, local copies, waits for them, and re-layouts: 7.5 us -> 0.01 us
    ppermute x0 -> x25, waiting for transfers between devices: none -> 6.66 us  [the longest x10 4.94 us: shifted(): lax.ppermute(array, name, [(i, (i + shift) % size) for i in range(size)])]
    pallas_call x1, Pallas kernels: 7.91 us -> 9.91 us  [body(): pl.pallas_call(functools.partial(transform_kernel, points), out_shape=jax...]
  transfers between devices with their start and end apart: 1 -> 26, of which waited for: 1 -> 5; matrix products, arithmetic and copies ran while one was open for 0% -> 0% of each run, Pallas kernels for 0% -> 0%
where the time goes in v2:
time: 164 us; the launch traced here: 163 us
  starting transfers between devices  129 us (79%)
  waiting for transfers between devices  22.2 us (14%)
  Pallas kernels  11.7 us (7%)
    ppermute x15, starting transfers between devices, body(): lax.ppermute(terms[partner], 'ga', [(i, i ^ partner) for i in range(group...  68.8 us
    ppermute x10, starting transfers between devices, shifted(): lax.ppermute(array, name, [(i, (i + shift) % size) for i in range(size)])  45.8 us
    all_to_all x1, waiting for transfers between devices, body(): lax.all_to_all(partial, 'ga', split_axis=0, concat_axis=0, tiled=True)  15.6 us
    all_to_all x1, starting transfers between devices, body(): lax.all_to_all(partial, 'ga', split_axis=0, concat_axis=0, tiled=True)  14.3 us
    pallas_call x1, Pallas kernels, body(): pl.pallas_call(functools.partial(transform_kernel, points), out_shape=jax...  9.91 us
    ppermute x10, waiting for transfers between devices, shifted(): lax.ppermute(array, name, [(i, (i + shift) % size) for i in range(size)])  4.94 us
  transfers between devices with their start and end apart: 26, of which 5 were waited for; matrix products, arithmetic and copies ran while one was open for 0% of the time, Pallas kernels for 0%

profile of v2, /device:TPU:1, one launch (start us, length us, event | category | flops | bytes accessed | tf_op | source)
XLA Modules:
  0.0 163.4 jit_solution(1934460862342865314)
XLA Ops:
  0.0 9.9 %transform.1 = f32[16,80,128]{2,1,0:T(8,128)} custom-call(s32[8]{0:T(128)} %valence_ids.1, s32[8]{0:T(128)} %conduct_ids.1, s32[1]{0:T(128)} %bitcast.position, bf16[2,16,128,128]{3,2,1,0:T(8,128)(2,1)} %bitcast.19, bf16[2,16,128,128]{3,2,1,0:T(8,128)(2,1)} %bitcast.20, bf16[2,128,128]{2,1,0:T(8,128)(2,1)} %bitcast.21, s32[80,128]{1,0:T(8,128)} %bitcast.22, ...), custom_call_target="tpu_custom_call" | custom-call | tf_op jit(solution)/shard_map/transform/pallas_call | solution.py:315
  9.9 14.3 %all-to-all-start = ((f32[16,80,128]{2,1,0:T(8,128)}), f32[16,80,128]{2,1,0:T(8,128)S(1)}, u32[]{:S(2)}, u32[]{:S(2)}) async-start(f32[16,80,128]{2,1,0:T(8,128)} %transform.1), calls=%async_computation | async-start | bytes 1310720 | tf_op jit(solution)/shard_map/all_to_all | solution.py:346
  24.2 15.6 %all-to-all-done.partial = f32[16,80,128]{2,1,0:T(8,128)S(1)} async-done(((f32[16,80,128]{2,1,0:T(8,128)}), f32[16,80,128]{2,1,0:T(8,128)S(1)}, u32[]{:S(2)}, u32[]{:S(2)}) %all-to-all-start) | async-done | bytes 655392 | tf_op jit(solution)/shard_map/all_to_all | solution.py:346
  39.8 3.2 %collective-permute-start = (bf16[80,128]{1,0:T(8,128)(2,1)S(1)}, bf16[80,128]{1,0:T(8,128)(2,1)S(1)}, u32[]{:S(2)}, u32[]{:S(2)}) collective-permute-start(bf16[80,128]{1,0:T(8,128)(2,1)S(1)} %weight.1.refs_0_.own), channel_id=1, source_target_pairs={{0,64},{64,128},{128,192},{192,256},{256,320},{320,384},{384,448},... | collective-permute-start | bytes 61448 | tf_op jit(solution)/shard_map/ppermute | solution.py:358
  43.0 4.2 %collective-permute-start.1 = (bf16[80,128]{1,0:T(8,128)(2,1)S(1)}, bf16[80,128]{1,0:T(8,128)(2,1)S(1)}, u32[]{:S(2)}, u32[]{:S(2)}) collective-permute-start(bf16[80,128]{1,0:T(8,128)(2,1)S(1)} %weight.1.refs_0_.own), channel_id=1, source_target_pairs={{0,128},{64,192},{128,256},{192,320},{256,384},{320,448},{384,0},{... | collective-permute-start | bytes 61448 | tf_op jit(solution)/shard_map/ppermute | solution.py:358
  47.3 4.6 %collective-permute-start.2 = (bf16[80,128]{1,0:T(8,128)(2,1)S(1)}, bf16[80,128]{1,0:T(8,128)(2,1)S(1)}, u32[]{:S(2)}, u32[]{:S(2)}) collective-permute-start(bf16[80,128]{1,0:T(8,128)(2,1)S(1)} %weight.1.refs_0_.own), channel_id=1, source_target_pairs={{0,192},{64,256},{128,320},{192,384},{256,448},{320,0},{384,64},{4... | collective-permute-start | bytes 61448 | tf_op jit(solution)/shard_map/ppermute | solution.py:358
  51.9 3.5 %collective-permute-start.3 = (bf16[80,128]{1,0:T(8,128)(2,1)S(1)}, bf16[80,128]{1,0:T(8,128)(2,1)S(1)}, u32[]{:S(2)}, u32[]{:S(2)}) collective-permute-start(bf16[80,128]{1,0:T(8,128)(2,1)S(1)} %weight.1.refs_0_.own), channel_id=1, source_target_pairs={{0,256},{64,320},{128,384},{192,448},{256,0},{320,64},{384,128},{4... | collective-permute-start | bytes 61448 | tf_op jit(solution)/shard_map/ppermute | solution.py:358
  55.5 4.9 %collective-permute-start.4 = (bf16[80,128]{1,0:T(8,128)(2,1)S(1)}, bf16[80,128]{1,0:T(8,128)(2,1)S(1)}, u32[]{:S(2)}, u32[]{:S(2)}) collective-permute-start(bf16[80,128]{1,0:T(8,128)(2,1)S(1)} %weight.1.refs_0_.own), channel_id=1, source_target_pairs={{0,320},{64,384},{128,448},{192,0},{256,64},{320,128},{384,192},{4... | collective-permute-start | bytes 61448 | tf_op jit(solution)/shard_map/ppermute | solution.py:358
  60.4 5.0 %collective-permute-start.5 = (bf16[80,128]{1,0:T(8,128)(2,1)S(1)}, bf16[80,128]{1,0:T(8,128)(2,1)S(1)}, u32[]{:S(2)}, u32[]{:S(2)}) collective-permute-start(bf16[80,128]{1,0:T(8,128)(2,1)S(1)} %weight.1.refs_0_.own), channel_id=1, source_target_pairs={{0,384},{64,448},{128,0},{192,64},{256,128},{320,192},{384,256},{4... | collective-permute-start | bytes 61448 | tf_op jit(solution)/shard_map/ppermute | solution.py:358
  65.3 3.0 %collective-permute-start.6 = (bf16[80,128]{1,0:T(8,128)(2,1)S(1)}, bf16[80,128]{1,0:T(8,128)(2,1)S(1)}, u32[]{:S(2)}, u32[]{:S(2)}) collective-permute-start(bf16[80,128]{1,0:T(8,128)(2,1)S(1)} %weight.1.refs_0_.own), channel_id=1, source_target_pairs={{0,448},{64,0},{128,64},{192,128},{256,192},{320,256},{384,320},{4... | collective-permute-start | bytes 61448 | tf_op jit(solution)/shard_map/ppermute | solution.py:358
  69.9 9.6 %collective-permute-start.7 = (bf16[8,80,128]{2,1,0:T(8,128)(2,1)S(1)}, bf16[8,80,128]{2,1,0:T(8,128)(2,1)S(1)}, u32[]{:S(2)}, u32[]{:S(2)}) collective-permute-start(bf16[8,80,128]{2,1,0:T(8,128)(2,1)S(1)} %stack.1.refs_0_), channel_id=1, source_target_pairs={{0,16},{16,32},{32,48},{48,0},{1,17},{17,33},{33,49},{49,1},{2,18}... | collective-permute-start | bytes 491528 | tf_op jit(solution)/shard_map/ppermute | solution.py:358
  79.6 3.5 %collective-permute-start.8 = (bf16[8,80,128]{2,1,0:T(8,128)(2,1)S(1)}, bf16[8,80,128]{2,1,0:T(8,128)(2,1)S(1)}, u32[]{:S(2)}, u32[]{:S(2)}) collective-permute-start(bf16[8,80,128]{2,1,0:T(8,128)(2,1)S(1)} %stack.1.refs_0_), channel_id=1, source_target_pairs={{0,32},{16,48},{32,0},{48,16},{1,33},{17,49},{33,1},{49,17},{2,34}... | collective-permute-start | bytes 491528 | tf_op jit(solution)/shard_map/ppermute | solution.py:358
  83.1 4.3 %collective-permute-start.9 = (bf16[8,80,128]{2,1,0:T(8,128)(2,1)S(1)}, bf16[8,80,128]{2,1,0:T(8,128)(2,1)S(1)}, u32[]{:S(2)}, u32[]{:S(2)}) collective-permute-start(bf16[8,80,128]{2,1,0:T(8,128)(2,1)S(1)} %stack.1.refs_0_), channel_id=1, source_target_pairs={{0,48},{16,0},{32,16},{48,32},{1,49},{17,1},{33,17},{49,33},{2,50}... | collective-permute-start | bytes 491528 | tf_op jit(solution)/shard_map/ppermute | solution.py:358
  92.0 6.2 %collective-permute-start.10 = (f32[16,128]{1,0:T(8,128)S(1)}, f32[16,128]{1,0:T(8,128)S(1)}, u32[]{:S(2)}, u32[]{:S(2)}) collective-permute-start(f32[16,128]{1,0:T(8,128)S(1)} %get-tuple-element.22), channel_id=1, source_target_pairs={{0,1},{1,0},{2,3},{3,2},{4,5},{5,4},{6,7},{7,6},{8,9},{9,8},{10,11... | collective-permute-start | bytes 24584 | tf_op jit(solution)/shard_map/ppermute | solution.py:383
  100.1 7.4 %collective-permute-start.12 = (f32[16,128]{1,0:T(8,128)S(1)}, f32[16,128]{1,0:T(8,128)S(1)}, u32[]{:S(2)}, u32[]{:S(2)}) collective-permute-start(f32[16,128]{1,0:T(8,128)S(1)} %get-tuple-element.24), channel_id=1, source_target_pairs={{0,3},{1,2},{2,1},{3,0},{4,7},{5,6},{6,5},{7,4},{8,11},{9,10},{10,... | collective-permute-start | bytes 24584 | tf_op jit(solution)/shard_map/ppermute | solution.py:383
  109.5 3.7 %collective-permute-start.14 = (f32[16,128]{1,0:T(8,128)S(1)}, f32[16,128]{1,0:T(8,128)S(1)}, u32[]{:S(2)}, u32[]{:S(2)}) collective-permute-start(f32[16,128]{1,0:T(8,128)S(1)} %get-tuple-element.26), channel_id=1, source_target_pairs={{0,5},{1,4},{2,7},{3,6},{4,1},{5,0},{6,3},{7,2},{8,13},{9,12},{10,... | collective-permute-start | bytes 24584 | tf_op jit(solution)/shard_map/ppermute | solution.py:383
  115.2 8.3 %collective-permute-start.16 = (f32[16,128]{1,0:T(8,128)S(1)}, f32[16,128]{1,0:T(8,128)S(1)}, u32[]{:S(2)}, u32[]{:S(2)}) collective-permute-start(f32[16,128]{1,0:T(8,128)S(1)} %get-tuple-element.28), channel_id=1, source_target_pairs={{0,7},{1,6},{2,5},{3,4},{4,3},{5,2},{6,1},{7,0},{8,15},{9,14},{10,... | collective-permute-start | bytes 24584 | tf_op jit(solution)/shard_map/ppermute | solution.py:383
  123.5 2.5 %collective-permute-start.17 = (f32[16,128]{1,0:T(8,128)S(1)}, f32[16,128]{1,0:T(8,128)S(1)}, u32[]{:S(2)}, u32[]{:S(2)}) collective-permute-start(f32[16,128]{1,0:T(8,128)S(1)} %get-tuple-element.29), channel_id=1, source_target_pairs={{0,8},{1,9},{2,10},{3,11},{4,12},{5,13},{6,14},{7,15},{8,0},{9,1},... | collective-permute-start | bytes 24584 | tf_op jit(solution)/shard_map/ppermute | solution.py:383
  126.0 4.7 %collective-permute-start.18 = (f32[16,128]{1,0:T(8,128)S(1)}, f32[16,128]{1,0:T(8,128)S(1)}, u32[]{:S(2)}, u32[]{:S(2)}) collective-permute-start(f32[16,128]{1,0:T(8,128)S(1)} %get-tuple-element.30), channel_id=1, source_target_pairs={{0,9},{1,8},{2,11},{3,10},{4,13},{5,12},{6,15},{7,14},{8,1},{9,0},... | collective-permute-start | bytes 24584 | tf_op jit(solution)/shard_map/ppermute | solution.py:383
  130.7 2.5 %collective-permute-start.19 = (f32[16,128]{1,0:T(8,128)S(1)}, f32[16,128]{1,0:T(8,128)S(1)}, u32[]{:S(2)}, u32[]{:S(2)}) collective-permute-start(f32[16,128]{1,0:T(8,128)S(1)} %get-tuple-element.31), channel_id=1, source_target_pairs={{0,10},{1,11},{2,8},{3,9},{4,14},{5,15},{6,12},{7,13},{8,2},{9,3},... | collective-permute-start | bytes 24584 | tf_op jit(solution)/shard_map/ppermute | solution.py:383
  133.3 9.3 %collective-permute-start.20 = (f32[16,128]{1,0:T(8,128)S(1)}, f32[16,128]{1,0:T(8,128)S(1)}, u32[]{:S(2)}, u32[]{:S(2)}) collective-permute-start(f32[16,128]{1,0:T(8,128)S(1)} %get-tuple-element.32), channel_id=1, source_target_pairs={{0,11},{1,10},{2,9},{3,8},{4,15},{5,14},{6,13},{7,12},{8,3},{9,2},... | collective-permute-start | bytes 24584 | tf_op jit(solution)/shard_map/ppermute | solution.py:383
  142.5 2.5 %collective-permute-start.21 = (f32[16,128]{1,0:T(8,128)S(1)}, f32[16,128]{1,0:T(8,128)S(1)}, u32[]{:S(2)}, u32[]{:S(2)}) collective-permute-start(f32[16,128]{1,0:T(8,128)S(1)} %get-tuple-element.33), channel_id=1, source_target_pairs={{0,12},{1,13},{2,14},{3,15},{4,8},{5,9},{6,10},{7,11},{8,4},{9,5},... | collective-permute-start | bytes 24584 | tf_op jit(solution)/shard_map/ppermute | solution.py:383
  145.0 4.4 %collective-permute-start.22 = (f32[16,128]{1,0:T(8,128)S(1)}, f32[16,128]{1,0:T(8,128)S(1)}, u32[]{:S(2)}, u32[]{:S(2)}) collective-permute-start(f32[16,128]{1,0:T(8,128)S(1)} %get-tuple-element.34), channel_id=1, source_target_pairs={{0,13},{1,12},{2,15},{3,14},{4,9},{5,8},{6,11},{7,10},{8,5},{9,4},... | collective-permute-start | bytes 24584 | tf_op jit(solution)/shard_map/ppermute | solution.py:383
  151.7 9.3 %collective-permute-start.24 = (f32[16,128]{1,0:T(8,128)S(1)}, f32[16,128]{1,0:T(8,128)S(1)}, u32[]{:S(2)}, u32[]{:S(2)}) collective-permute-start(f32[16,128]{1,0:T(8,128)S(1)} %get-tuple-element.36), channel_id=1, source_target_pairs={{0,15},{1,14},{2,13},{3,12},{4,11},{5,10},{6,9},{7,8},{8,7},{9,6},... | collective-permute-start | bytes 24584 | tf_op jit(solution)/shard_map/ppermute | solution.py:383
  (37 shorter events, 16.6 us)
Async XLA Ops:
  9.9 29.9 %all-to-all-start = ((f32[16,80,128]{2,1,0:T(8,128)}), f32[16,80,128]{2,1,0:T(8,128)S(1)}, u32[]{:S(2)}, u32[]{:S(2)}) async-start(f32[16,80,128]{2,1,0:T(8,128)} %transform.1), calls=%async_computation | async-start | bytes 1310720 | tf_op jit(solution)/shard_map/all_to_all | solution.py:346
  39.8 20.5 %collective-permute-start = (bf16[80,128]{1,0:T(8,128)(2,1)S(1)}, bf16[80,128]{1,0:T(8,128)(2,1)S(1)}, u32[]{:S(2)}, u32[]{:S(2)}) collective-permute-start(bf16[80,128]{1,0:T(8,128)(2,1)S(1)} %weight.1.refs_0_.own), channel_id=1, source_target_pairs={{0,64},{64,128},{128,192},{192,256},{256,320},{320,384},{384,448},... | collective-permute-start | bytes 61448 | tf_op jit(solution)/shard_map/ppermute | solution.py:358
  43.0 22.3 %collective-permute-start.1 = (bf16[80,128]{1,0:T(8,128)(2,1)S(1)}, bf16[80,128]{1,0:T(8,128)(2,1)S(1)}, u32[]{:S(2)}, u32[]{:S(2)}) collective-permute-start(bf16[80,128]{1,0:T(8,128)(2,1)S(1)} %weight.1.refs_0_.own), channel_id=1, source_target_pairs={{0,128},{64,192},{128,256},{192,320},{256,384},{320,448},{384,0},{... | collective-permute-start | bytes 61448 | tf_op jit(solution)/shard_map/ppermute | solution.py:358
  47.3 21.1 %collective-permute-start.2 = (bf16[80,128]{1,0:T(8,128)(2,1)S(1)}, bf16[80,128]{1,0:T(8,128)(2,1)S(1)}, u32[]{:S(2)}, u32[]{:S(2)}) collective-permute-start(bf16[80,128]{1,0:T(8,128)(2,1)S(1)} %weight.1.refs_0_.own), channel_id=1, source_target_pairs={{0,192},{64,256},{128,320},{192,384},{256,448},{320,0},{384,64},{4... | collective-permute-start | bytes 61448 | tf_op jit(solution)/shard_map/ppermute | solution.py:358
  51.9 16.4 %collective-permute-start.3 = (bf16[80,128]{1,0:T(8,128)(2,1)S(1)}, bf16[80,128]{1,0:T(8,128)(2,1)S(1)}, u32[]{:S(2)}, u32[]{:S(2)}) collective-permute-start(bf16[80,128]{1,0:T(8,128)(2,1)S(1)} %weight.1.refs_0_.own), channel_id=1, source_target_pairs={{0,256},{64,320},{128,384},{192,448},{256,0},{320,64},{384,128},{4... | collective-permute-start | bytes 61448 | tf_op jit(solution)/shard_map/ppermute | solution.py:358
  55.5 12.9 %collective-permute-start.4 = (bf16[80,128]{1,0:T(8,128)(2,1)S(1)}, bf16[80,128]{1,0:T(8,128)(2,1)S(1)}, u32[]{:S(2)}, u32[]{:S(2)}) collective-permute-start(bf16[80,128]{1,0:T(8,128)(2,1)S(1)} %weight.1.refs_0_.own), channel_id=1, source_target_pairs={{0,320},{64,384},{128,448},{192,0},{256,64},{320,128},{384,192},{4... | collective-permute-start | bytes 61448 | tf_op jit(solution)/shard_map/ppermute | solution.py:358
  60.4 8.0 %collective-permute-start.5 = (bf16[80,128]{1,0:T(8,128)(2,1)S(1)}, bf16[80,128]{1,0:T(8,128)(2,1)S(1)}, u32[]{:S(2)}, u32[]{:S(2)}) collective-permute-start(bf16[80,128]{1,0:T(8,128)(2,1)S(1)} %weight.1.refs_0_.own), channel_id=1, source_target_pairs={{0,384},{64,448},{128,0},{192,64},{256,128},{320,192},{384,256},{4... | collective-permute-start | bytes 61448 | tf_op jit(solution)/shard_map/ppermute | solution.py:358
  69.9 17.5 %collective-permute-start.7 = (bf16[8,80,128]{2,1,0:T(8,128)(2,1)S(1)}, bf16[8,80,128]{2,1,0:T(8,128)(2,1)S(1)}, u32[]{:S(2)}, u32[]{:S(2)}) collective-permute-start(bf16[8,80,128]{2,1,0:T(8,128)(2,1)S(1)} %stack.1.refs_0_), channel_id=1, source_target_pairs={{0,16},{16,32},{32,48},{48,0},{1,17},{17,33},{33,49},{49,1},{2,18}... | collective-permute-start | bytes 491528 | tf_op jit(solution)/shard_map/ppermute | solution.py:358
  79.6 9.5 %collective-permute-start.8 = (bf16[8,80,128]{2,1,0:T(8,128)(2,1)S(1)}, bf16[8,80,128]{2,1,0:T(8,128)(2,1)S(1)}, u32[]{:S(2)}, u32[]{:S(2)}) collective-permute-start(bf16[8,80,128]{2,1,0:T(8,128)(2,1)S(1)} %stack.1.refs_0_), channel_id=1, source_target_pairs={{0,32},{16,48},{32,0},{48,16},{1,33},{17,49},{33,1},{49,17},{2,34}... | collective-permute-start | bytes 491528 | tf_op jit(solution)/shard_map/ppermute | solution.py:358
  92.0 21.3 %collective-permute-start.10 = (f32[16,128]{1,0:T(8,128)S(1)}, f32[16,128]{1,0:T(8,128)S(1)}, u32[]{:S(2)}, u32[]{:S(2)}) collective-permute-start(f32[16,128]{1,0:T(8,128)S(1)} %get-tuple-element.22), channel_id=1, source_target_pairs={{0,1},{1,0},{2,3},{3,2},{4,5},{5,4},{6,7},{7,6},{8,9},{9,8},{10,11... | collective-permute-start | bytes 24584 | tf_op jit(solution)/shard_map/ppermute | solution.py:383
  98.2 17.0 %collective-permute-start.11 = (f32[16,128]{1,0:T(8,128)S(1)}, f32[16,128]{1,0:T(8,128)S(1)}, u32[]{:S(2)}, u32[]{:S(2)}) collective-permute-start(f32[16,128]{1,0:T(8,128)S(1)} %get-tuple-element.23), channel_id=1, source_target_pairs={{0,2},{1,3},{2,0},{3,1},{4,6},{5,7},{6,4},{7,5},{8,10},{9,11},{10,... | collective-permute-start | bytes 24584 | tf_op jit(solution)/shard_map/ppermute | solution.py:383
  100.1 23.4 %collective-permute-start.12 = (f32[16,128]{1,0:T(8,128)S(1)}, f32[16,128]{1,0:T(8,128)S(1)}, u32[]{:S(2)}, u32[]{:S(2)}) collective-permute-start(f32[16,128]{1,0:T(8,128)S(1)} %get-tuple-element.24), channel_id=1, source_target_pairs={{0,3},{1,2},{2,1},{3,0},{4,7},{5,6},{6,5},{7,4},{8,11},{9,10},{10,... | collective-permute-start | bytes 24584 | tf_op jit(solution)/shard_map/ppermute | solution.py:383
  107.5 18.5 %collective-permute-start.13 = (f32[16,128]{1,0:T(8,128)S(1)}, f32[16,128]{1,0:T(8,128)S(1)}, u32[]{:S(2)}, u32[]{:S(2)}) collective-permute-start(f32[16,128]{1,0:T(8,128)S(1)} %get-tuple-element.25), channel_id=1, source_target_pairs={{0,4},{1,5},{2,6},{3,7},{4,0},{5,1},{6,2},{7,3},{8,12},{9,13},{10,... | collective-permute-start | bytes 24584 | tf_op jit(solution)/shard_map/ppermute | solution.py:383
  109.5 21.3 %collective-permute-start.14 = (f32[16,128]{1,0:T(8,128)S(1)}, f32[16,128]{1,0:T(8,128)S(1)}, u32[]{:S(2)}, u32[]{:S(2)}) collective-permute-start(f32[16,128]{1,0:T(8,128)S(1)} %get-tuple-element.26), channel_id=1, source_target_pairs={{0,5},{1,4},{2,7},{3,6},{4,1},{5,0},{6,3},{7,2},{8,13},{9,12},{10,... | collective-permute-start | bytes 24584 | tf_op jit(solution)/shard_map/ppermute | solution.py:383
  113.2 20.0 %collective-permute-start.15 = (f32[16,128]{1,0:T(8,128)S(1)}, f32[16,128]{1,0:T(8,128)S(1)}, u32[]{:S(2)}, u32[]{:S(2)}) collective-permute-start(f32[16,128]{1,0:T(8,128)S(1)} %get-tuple-element.27), channel_id=1, source_target_pairs={{0,6},{1,7},{2,4},{3,5},{4,2},{5,3},{6,0},{7,1},{8,14},{9,15},{10,... | collective-permute-start | bytes 24584 | tf_op jit(solution)/shard_map/ppermute | solution.py:383
  115.2 27.4 %collective-permute-start.16 = (f32[16,128]{1,0:T(8,128)S(1)}, f32[16,128]{1,0:T(8,128)S(1)}, u32[]{:S(2)}, u32[]{:S(2)}) collective-permute-start(f32[16,128]{1,0:T(8,128)S(1)} %get-tuple-element.28), channel_id=1, source_target_pairs={{0,7},{1,6},{2,5},{3,4},{4,3},{5,2},{6,1},{7,0},{8,15},{9,14},{10,... | collective-permute-start | bytes 24584 | tf_op jit(solution)/shard_map/ppermute | solution.py:383
  123.5 21.5 %collective-permute-start.17 = (f32[16,128]{1,0:T(8,128)S(1)}, f32[16,128]{1,0:T(8,128)S(1)}, u32[]{:S(2)}, u32[]{:S(2)}) collective-permute-start(f32[16,128]{1,0:T(8,128)S(1)} %get-tuple-element.29), channel_id=1, source_target_pairs={{0,8},{1,9},{2,10},{3,11},{4,12},{5,13},{6,14},{7,15},{8,0},{9,1},... | collective-permute-start | bytes 24584 | tf_op jit(solution)/shard_map/ppermute | solution.py:383
  126.0 23.4 %collective-permute-start.18 = (f32[16,128]{1,0:T(8,128)S(1)}, f32[16,128]{1,0:T(8,128)S(1)}, u32[]{:S(2)}, u32[]{:S(2)}) collective-permute-start(f32[16,128]{1,0:T(8,128)S(1)} %get-tuple-element.30), channel_id=1, source_target_pairs={{0,9},{1,8},{2,11},{3,10},{4,13},{5,12},{6,15},{7,14},{8,1},{9,0},... | collective-permute-start | bytes 24584 | tf_op jit(solution)/shard_map/ppermute | solution.py:383
  130.7 20.9 %collective-permute-start.19 = (f32[16,128]{1,0:T(8,128)S(1)}, f32[16,128]{1,0:T(8,128)S(1)}, u32[]{:S(2)}, u32[]{:S(2)}) collective-permute-start(f32[16,128]{1,0:T(8,128)S(1)} %get-tuple-element.31), channel_id=1, source_target_pairs={{0,10},{1,11},{2,8},{3,9},{4,14},{5,15},{6,12},{7,13},{8,2},{9,3},... | collective-permute-start | bytes 24584 | tf_op jit(solution)/shard_map/ppermute | solution.py:383
  133.3 27.7 %collective-permute-start.20 = (f32[16,128]{1,0:T(8,128)S(1)}, f32[16,128]{1,0:T(8,128)S(1)}, u32[]{:S(2)}, u32[]{:S(2)}) collective-permute-start(f32[16,128]{1,0:T(8,128)S(1)} %get-tuple-element.32), channel_id=1, source_target_pairs={{0,11},{1,10},{2,9},{3,8},{4,15},{5,14},{6,13},{7,12},{8,3},{9,2},... | collective-permute-start | bytes 24584 | tf_op jit(solution)/shard_map/ppermute | solution.py:383
  142.5 18.4 %collective-permute-start.21 = (f32[16,128]{1,0:T(8,128)S(1)}, f32[16,128]{1,0:T(8,128)S(1)}, u32[]{:S(2)}, u32[]{:S(2)}) collective-permute-start(f32[16,128]{1,0:T(8,128)S(1)} %get-tuple-element.33), channel_id=1, source_target_pairs={{0,12},{1,13},{2,14},{3,15},{4,8},{5,9},{6,10},{7,11},{8,4},{9,5},... | collective-permute-start | bytes 24584 | tf_op jit(solution)/shard_map/ppermute | solution.py:383
  145.0 15.9 %collective-permute-start.22 = (f32[16,128]{1,0:T(8,128)S(1)}, f32[16,128]{1,0:T(8,128)S(1)}, u32[]{:S(2)}, u32[]{:S(2)}) collective-permute-start(f32[16,128]{1,0:T(8,128)S(1)} %get-tuple-element.34), channel_id=1, source_target_pairs={{0,13},{1,12},{2,15},{3,14},{4,9},{5,8},{6,11},{7,10},{8,5},{9,4},... | collective-permute-start | bytes 24584 | tf_op jit(solution)/shard_map/ppermute | solution.py:383
  149.5 11.5 %collective-permute-start.23 = (f32[16,128]{1,0:T(8,128)S(1)}, f32[16,128]{1,0:T(8,128)S(1)}, u32[]{:S(2)}, u32[]{:S(2)}) collective-permute-start(f32[16,128]{1,0:T(8,128)S(1)} %get-tuple-element.35), channel_id=1, source_target_pairs={{0,14},{1,15},{2,12},{3,13},{4,10},{5,11},{6,8},{7,9},{8,6},{9,7},... | collective-permute-start | bytes 24584 | tf_op jit(solution)/shard_map/ppermute | solution.py:383
  151.7 11.0 %collective-permute-start.24 = (f32[16,128]{1,0:T(8,128)S(1)}, f32[16,128]{1,0:T(8,128)S(1)}, u32[]{:S(2)}, u32[]{:S(2)}) collective-permute-start(f32[16,128]{1,0:T(8,128)S(1)} %get-tuple-element.36), channel_id=1, source_target_pairs={{0,15},{1,14},{2,13},{3,12},{4,11},{5,10},{6,9},{7,8},{8,7},{9,6},... | collective-permute-start | bytes 24584 | tf_op jit(solution)/shard_map/ppermute | solution.py:383
  (3 other events, 26.6 us)

commit v3 on v2

--- a/solution.py
+++ b/solution.py
@@ -90,8 +90,8 @@
     arrived,
 ):
     rows = points // 2 * SLAB
-    tiles = grid.shape[0] // out.shape[0]
-    blocks = out.shape[0]
+    blocks = out.shape[0] // 2
+    tiles = grid.shape[0] // blocks
     dot = functools.partial(jnp.dot, preferred_element_type=jnp.float32)
 
     copies = []
@@ -172,6 +172,7 @@
             field[1, start : start + rows] = pltpu.roll(turned_imag, points, 1) + sign * turned_imag
 
     half = blocks // 2
+    left = lane[:COUNT] < points
 
     def one_pair(k, carry):
         picked = []
@@ -221,73 +222,93 @@
                     sine = waves[2 * x + 1, pl.ds(row, 1), :]
                     total_real += pieces[0] * cosine + pieces[1] * sine
                     total_imag += pieces[1] * cosine - pieces[0] * sine
-                out[block, j * 2 * COUNT : (j * 2 + 1) * COUNT] = total_real.astype(out.dtype)
-                out[block, (j * 2 + 1) * COUNT : (j * 2 + 2) * COUNT] = total_imag.astype(out.dtype)
+                low = jnp.where(left, total_real, pltpu.roll(total_imag, points, 1))
+                high = jnp.where(left, pltpu.roll(total_real, points, 1), total_imag)
+                out[block, j * COUNT : (j + 1) * COUNT] = low
+                out[blocks + block, j * COUNT : (j + 1) * COUNT] = high
         return carry
 
     lax.fori_loop(0, half, one_pair, 0)
 
 
-def weight_kernel(scale, partial, coulomb, out):
-    total = partial[0].astype(jnp.float32)
+def weight_kernel(scale, side, partial, coulomb, out):
+    half = partial.shape[0] // 2
+    lane = lax.broadcasted_iota(jnp.int32, (COUNT, LANES), 1)
+    own = jnp.where(lane < LANES // 2, 0, 1) == (side[0] & 1)
+    factors = []
+    for j in range(partial.shape[1] // COUNT):
+        root = jnp.sqrt(coulomb[:, j * LANES : (j + 1) * LANES])
+        root = jnp.broadcast_to(root, (COUNT, LANES))
+        factors.append(jnp.where(own, root, pltpu.roll(root, LANES // 2, 1)))
+    factor = jnp.concatenate(factors, axis=0)
+    pieces = []
+    for first in (0, half):
+        total = partial[first]
+        for source in range(first + 1, first + half):
+            total += partial[source]
+        pieces.append((total * scale) * factor)
+    weighted = jnp.concatenate(pieces, axis=0).astype(jnp.bfloat16)
+    for target in range(out.shape[0]):
+        out[target] = weighted
+
+
+def panel_kernel(width, position, line_index, chip, gathered, out):
+    line, group = line_index[0], (chip[0] >> 1) ^ ((position[0] >> 1) & 1)
+    senders, height = gathered.shape[0], gathered.shape[1] // 2
+    tiles = height // COUNT
+    lane = lax.broadcasted_iota(jnp.int32, (1, LANES), 1)
+    sign = jnp.where(lane < LANES // 2, -1.0, 1.0).astype(jnp.float32)
+
+    def by_tile(array):
+        shape = array.shape[:-2] + (2, tiles, COUNT, LANES)
+        array = array.astype(jnp.float32).reshape(shape)
+        return [array[..., j, :, :].reshape(-1, LANES) for j in range(tiles)]
+
+    right = [tile.astype(jnp.bfloat16) for tile in by_tile(gathered[...])]
+    rows = jnp.stack([gathered[2 * line + group], gathered[2 * line + 1 - group]])
+    left = []
+    for tile in by_tile(rows):
+        turned = pltpu.roll(tile, LANES // 2, 1) * sign
+        left.append(jnp.concatenate([tile, turned], axis=0).astype(jnp.bfloat16))
+    total = lax.dot_general(
+        jnp.concatenate(left, axis=1),
+        jnp.concatenate(right, axis=1),
+        (((1,), (1,)), ((), ())),
+        preferred_element_type=jnp.float32,
+    )
+    out[...] = jnp.zeros_like(out)
+    count = 4 * COUNT
+    slot = 0
+    for far in range(2):
+        for side in range(2):
+            start = (2 * far + side) * COUNT
+            real = total[start : start + COUNT]
+            imag = total[count + start : count + start + COUNT]
+            for column in last_columns(out.shape[0] // 2, far):
+                at = slice(column * width, (column + 1) * width)
+                out[slot, :, :width] = real[:, at]
+                out[slot, :, LANES // 2 : LANES // 2 + width] = imag[:, at]
+                slot += 1
+
+
+def sum_kernel(scale, partial, out):
+    total = partial[0]
     for source in range(1, partial.shape[0]):
-        total += partial[source].astype(jnp.float32)
-    root = jnp.sqrt(coulomb[...])
-    height = 2 * COUNT
-    pieces = []
-    for j in range(total.shape[0] // height):
-        factor = root[:, j * LANES : (j + 1) * LANES]
-        pieces.append((total[j * height : (j + 1) * height] * scale) * factor)
-    out[...] = jnp.concatenate(pieces, axis=0).astype(jnp.bfloat16)
-
-
-def stack_kernel(position, *refs):
-    pieces, out = refs[:-1], refs[-1]
-    for shift, piece in enumerate(pieces):
-        out[(position[0] - shift + len(pieces)) % len(pieces)] = piece[...]
-
-
-def panel_kernel(place, own, *refs):
-    tcs = place[1]
-    chips = lax.axis_size("tc")
-    stacks, outs, (gathered, terms) = refs[:chips], refs[chips:-2], refs[-2:]
-    lines = stacks[0].shape[0]
-    for shift, stack in enumerate(stacks):
-        line = (tcs - shift + chips) % chips
-        for other in range(lines):
-            gathered[other * chips + line] = stack[other]
-    senders, height = lines * chips, 2 * COUNT
-    tiles = gathered.shape[1] // height
-    first, second, right = [], [], []
-    for j in range(tiles):
-        left = own[j * height : (j + 1) * height].astype(jnp.float32)
-        real, imag = left[:COUNT], left[COUNT:]
-        empty = jnp.zeros((LANES - height, LANES), jnp.float32)
-        first.append(jnp.concatenate([real, -imag, empty], axis=0).astype(jnp.bfloat16))
-        second.append(jnp.concatenate([imag, real, empty], axis=0).astype(jnp.bfloat16))
-        right.append(gathered[:, j * height : (j + 1) * height].reshape(senders * height, LANES))
-    right = jnp.concatenate(right, axis=1)
-    contract = (((1,), (1,)), ((), ()))
-
-    def product(left):
-        result = lax.dot_general(
-            right, jnp.concatenate(left, axis=1), contract, preferred_element_type=jnp.float32
-        )
-        return result.reshape(senders, 2, COUNT, LANES)
-
-    total = product(first)[:, 0] + product(second)[:, 1]
-    terms[...] = total.reshape(terms.shape)
-    for partner, out in enumerate(outs):
-        out[...] = terms[place[0] ^ partner]
-
-
-def sum_kernel(scale, *refs):
-    out = refs[-1]
-    total = refs[0][...]
-    for piece in refs[1:-1]:
-        total += piece[...]
-    turned = (total * scale).T[: 2 * COUNT]
-    out[...] = turned[:, : out.shape[2]].reshape(out.shape)
+        total += partial[source]
+    total *= scale
+    width = out.shape[2]
+    out[0] = total[:, :width]
+    out[1] = total[:, LANES // 2 : LANES // 2 + width]
+
+
+def last_columns(groups, far):
+    return [g for g in range(groups) if (g // 2) % 2 == far]
+
+
+def exchange(array, names, groups):
+    return lax.all_to_all(
+        array, names, split_axis=0, concat_axis=0, tiled=True, axis_index_groups=groups
+    )
 
 
 def body(valence, conduction, envelope, valence_index, conduction_index, grid_index, coulomb):
@@ -296,7 +317,7 @@
     per_device = coulomb.shape[0]
     tiles = per_device // LANES
     rows = points // 2 * SLAB
-    height = tiles * 2 * COUNT
+    height = tiles * COUNT
     width = lines * chips * COUNT // groups
 
     def turned(array):
@@ -311,10 +332,29 @@
     vmem = pl.BlockSpec(memory_space=pltpu.VMEM)
     anywhere = pl.BlockSpec(memory_space=pl.ANY)
     limit = pltpu.CompilerParams(vmem_limit_bytes=16 * 1024 * 1024)
+
+    by_planes = [
+        [(2 * high + low) * groups + g for low in range(2) for g in range(groups)]
+        for high in range(chips // 2)
+    ]
+    by_rows = [
+        [i * chips + 2 * high + low for i in range(lines) for high in range(chips // 2)]
+        for low in range(2)
+    ]
+    by_columns = [
+        [
+            (2 * (high ^ far) + low) * groups + g
+            for far in range(2)
+            for low in range(2)
+            for g in last_columns(groups, far)
+        ]
+        for high in range(chips // 2)
+    ]
+
     along_z, along_y, twist = tables(points)
     partial = pl.pallas_call(
         functools.partial(transform_kernel, points),
-        out_shape=jax.ShapeDtypeStruct((groups, height, LANES), jnp.float32),
+        out_shape=jax.ShapeDtypeStruct((2 * groups, height, LANES), jnp.float32),
         in_specs=[smem] * 3 + [anywhere] * 7,
         out_specs=vmem,
         scratch_shapes=[
@@ -343,54 +383,33 @@
         along_y,
         twist,
     )
-    partial = lax.all_to_all(partial, "ga", split_axis=0, concat_axis=0, tiled=True)
-    own = pl.pallas_call(
+    partial = exchange(partial, ("tc", "ga"), by_planes)
+    copies = pl.pallas_call(
         functools.partial(weight_kernel, float(points) ** -1.5),
-        out_shape=jax.ShapeDtypeStruct((height, LANES), jnp.bfloat16),
-        in_specs=[vmem] * 2,
+        out_shape=jax.ShapeDtypeStruct((lines * chips // 2, 2 * height, LANES), jnp.bfloat16),
+        in_specs=[smem, vmem, vmem],
         out_specs=vmem,
         compiler_params=limit,
         name="weight",
-    )(partial, coulomb.reshape(1, per_device))
-
-    def shifted(array, name, shift):
-        size = lax.axis_size(name)
-        return lax.ppermute(array, name, [(i, (i + shift) % size) for i in range(size)])
-
-    pieces = [own] + [shifted(own, "tr", shift) for shift in range(1, lines)]
-    stack = pl.pallas_call(
-        stack_kernel,
-        out_shape=jax.ShapeDtypeStruct((lines, height, LANES), jnp.bfloat16),
-        in_specs=[smem] + [vmem] * lines,
+    )(chip, partial, coulomb.reshape(1, per_device))
+    gathered = exchange(copies, ("tr", "tc"), by_rows)
+    terms = pl.pallas_call(
+        functools.partial(panel_kernel, width),
+        out_shape=jax.ShapeDtypeStruct((2 * groups, COUNT, LANES), jnp.float32),
+        in_specs=[smem] * 3 + [vmem],
         out_specs=vmem,
         compiler_params=limit,
-        name="stack",
-    )(line, *pieces)
-    stacks = [stack] + [shifted(stack, "tc", shift) for shift in range(1, chips)]
-    terms = pl.pallas_call(
-        panel_kernel,
-        out_shape=[jax.ShapeDtypeStruct((width, LANES), jnp.float32)] * groups,
-        in_specs=[smem] + [vmem] * (1 + chips),
-        out_specs=[vmem] * groups,
-        scratch_shapes=[
-            pltpu.VMEM((lines * chips, height, LANES), jnp.bfloat16),
-            pltpu.VMEM((groups, width, LANES), jnp.float32),
-        ],
-        compiler_params=limit,
         name="panel",
-    )(jnp.concatenate([position, chip]), own, *stacks)
-    pieces = [terms[0]] + [
-        lax.ppermute(terms[partner], "ga", [(i, i ^ partner) for i in range(groups)])
-        for partner in range(1, groups)
-    ]
+    )(position, line, chip, gathered)
+    terms = exchange(terms, ("tc", "ga"), by_columns)
     return pl.pallas_call(
         functools.partial(sum_kernel, 1.0 / (per_device * groups)),
         out_shape=jax.ShapeDtypeStruct((2, COUNT, width), jnp.float32),
-        in_specs=[vmem] * groups,
+        in_specs=[vmem],
         out_specs=vmem,
         compiler_params=limit,
         name="total",
-    )(*pieces)
+    )(terms)
 
 
 def solution(mesh):

time: 164 us -> 84.3 us (0.51)
  starting transfers between devices: 129 us -> 26.6 us
  blocking collectives: 0 us -> 13.5 us
  waiting for transfers between devices: 22.2 us -> 30.8 us
    ppermute x25 -> x0, starting transfers between devices: 115 us -> none  [the longest x15 68.8 us: body(): lax.ppermute(terms[partner], 'ga', [(i, i ^ partner) for i in range(group...]
    all_to_all x1 -> x2, waiting for transfers between devices: 15.6 us -> 30.8 us  [exchange(): lax.all_to_all(array, names, split_axis=0, concat_axis=0, tiled=True, axi...]
    all_to_all x0 -> x1, blocking collectives: none -> 13.5 us  [exchange(): lax.all_to_all(array, names, split_axis=0, concat_axis=0, tiled=True, axi...]
    all_to_all x1 -> x2, starting transfers between devices: 14.3 us -> 26.6 us  [exchange(): lax.all_to_all(array, names, split_axis=0, concat_axis=0, tiled=True, axi...]
    ppermute x25 -> x0, waiting for transfers between devices: 6.66 us -> none  [the longest x10 4.94 us: shifted(): lax.ppermute(array, name, [(i, (i + shift) % size) for i in range(size)])]
  transfers between devices with their start and end apart: 26 -> 2, of which waited for: 5 -> 2; matrix products, arithmetic and copies ran while one was open for 0% -> 0% of each run, Pallas kernels for 0% -> 0%
where the time goes in v3:
time: 84.3 us; the launch traced here: 84 us
  waiting for transfers between devices  30.8 us (37%)
  starting transfers between devices  26.6 us (32%)
  blocking collectives  13.5 us (16%)
  Pallas kernels  12.3 us (15%)
    all_to_all x2, waiting for transfers between devices, exchange(): lax.all_to_all(array, names, split_axis=0, concat_axis=0, tiled=True, axi...  30.8 us
    all_to_all x2, starting transfers between devices, exchange(): lax.all_to_all(array, names, split_axis=0, concat_axis=0, tiled=True, axi...  26.6 us
    all_to_all x1, blocking collectives, exchange(): lax.all_to_all(array, names, split_axis=0, concat_axis=0, tiled=True, axi...  13.5 us
    pallas_call x1, Pallas kernels, body(): pl.pallas_call(functools.partial(transform_kernel, points), out_shape=jax...  10.5 us
  transfers between devices with their start and end apart: 2, of which 2 were waited for; matrix products, arithmetic and copies ran while one was open for 0% of the time, Pallas kernels for 0%

profile of v3, /device:TPU:1, one launch (start us, length us, event | category | flops | bytes accessed | tf_op | source)
XLA Modules:
  0.0 84.0 jit_solution(10287880521873774808)
XLA Ops:
  0.0 10.5 %transform.1 = f32[32,40,128]{2,1,0:T(8,128)} custom-call(s32[8]{0:T(128)} %valence_ids.1, s32[8]{0:T(128)} %conduct_ids.1, s32[1]{0:T(128)} %bitcast.position, bf16[2,16,128,128]{3,2,1,0:T(8,128)(2,1)} %bitcast.19, bf16[2,16,128,128]{3,2,1,0:T(8,128)(2,1)} %bitcast.20, bf16[2,128,128]{2,1,0:T(8,128)(2,1)} %bitcast.21, s32[80,128]{1,0:T(8,128)} %bitcast.22, ...), custom_call_target="tpu_custom_call" | custom-call | tf_op jit(solution)/shard_map/transform/pallas_call | solution.py:355
  10.5 14.4 %all-to-all-start = ((f32[32,40,128]{2,1,0:T(8,128)}), f32[32,40,128]{2,1,0:T(8,128)S(1)}, u32[]{:S(2)}, u32[]{:S(2)}) async-start(f32[32,40,128]{2,1,0:T(8,128)} %transform.1), calls=%async_computation | async-start | bytes 1310720 | tf_op jit(solution)/shard_map/all_to_all | solution.py:309
  24.9 0.0 copy-start
  24.9 0.7 copy-done
  25.6 17.6 %all-to-all-done.partial = f32[32,40,128]{2,1,0:T(8,128)S(1)} async-done(((f32[32,40,128]{2,1,0:T(8,128)}), f32[32,40,128]{2,1,0:T(8,128)S(1)}, u32[]{:S(2)}, u32[]{:S(2)}) %all-to-all-start) | async-done | bytes 655392 | tf_op jit(solution)/shard_map/all_to_all | solution.py:309
  43.2 0.8 weight.1
  44.0 12.2 %all-to-all-start.1 = ((bf16[16,80,128]{2,1,0:T(8,128)(2,1)}), bf16[16,80,128]{2,1,0:T(8,128)(2,1)S(1)}, u32[]{:S(2)}, u32[]{:S(2)}) async-start(bf16[16,80,128]{2,1,0:T(8,128)(2,1)} %weight.1), calls=%async_computation.1 | async-start | bytes 655360 | tf_op jit(solution)/shard_map/all_to_all | solution.py:309
  56.2 13.2 %all-to-all-done.1.gathered = bf16[16,80,128]{2,1,0:T(8,128)(2,1)S(1)} async-done(((bf16[16,80,128]{2,1,0:T(8,128)(2,1)}), bf16[16,80,128]{2,1,0:T(8,128)(2,1)S(1)}, u32[]{:S(2)}, u32[]{:S(2)}) %all-to-all-start.1) | async-done | bytes 327712 | tf_op jit(solution)/shard_map/all_to_all | solution.py:309
  69.4 0.3 panel.1
  69.8 13.5 %all_to_all.15.partial = f32[32,8,128]{2,1,0:T(8,128)S(1)} all-to-all(f32[32,8,128]{2,1,0:T(8,128)S(1)} %panel.1), channel_id=1, replica_groups={{0,1,4,5,8,9,12,13,16,17,20,21,24,25,28,29,34,35,38,39,42,43,46,47,50,5..., dimensions={0} | all-to-all | bytes 262144 | tf_op jit(solution)/shard_map/all_to_all | solution.py:309
  83.3 0.7 total.1
  (1 shorter events, 0.0 us)
Async XLA Ops:
  10.5 32.7 %all-to-all-start = ((f32[32,40,128]{2,1,0:T(8,128)}), f32[32,40,128]{2,1,0:T(8,128)S(1)}, u32[]{:S(2)}, u32[]{:S(2)}) async-start(f32[32,40,128]{2,1,0:T(8,128)} %transform.1), calls=%async_computation | async-start | bytes 1310720 | tf_op jit(solution)/shard_map/all_to_all | solution.py:309
  24.9 0.7 copy-start
  44.0 25.4 %all-to-all-start.1 = ((bf16[16,80,128]{2,1,0:T(8,128)(2,1)}), bf16[16,80,128]{2,1,0:T(8,128)(2,1)S(1)}, u32[]{:S(2)}, u32[]{:S(2)}) async-start(bf16[16,80,128]{2,1,0:T(8,128)(2,1)} %weight.1), calls=%async_computation.1 | async-start | bytes 655360 | tf_op jit(solution)/shard_map/all_to_all | solution.py:309

commit v4 on v3

--- a/solution.py
+++ b/solution.py
@@ -87,6 +87,7 @@
     twist,
     field,
     waves,
+    powers,
     arrived,
 ):
     rows = points // 2 * SLAB
@@ -132,6 +133,7 @@
     for copy in whole[1:]:
         copy.wait()
     z_high, z_low = halves(along_z[...])
+    z_both = jnp.concatenate([z_high, z_high], axis=0)
     y_high, y_low = halves(along_y[...])
 
     common_real = common[0].astype(jnp.float32)
@@ -149,8 +151,12 @@
             right_imag = right_rows[t, 1].astype(jnp.float32) + common_imag
             parts.append(left_real * right_real + left_imag * right_imag)
             parts.append(left_real * right_imag - left_imag * right_real)
+            peak = jnp.max(jnp.maximum(jnp.abs(parts[-2]), jnp.abs(parts[-1])), axis=0, keepdims=True)
+            peak = jnp.max(peak, axis=1, keepdims=True)
+            power = jnp.clip(jnp.ceil(jnp.log2(peak)), -120.0, 120.0)
+            powers[t : t + 1] = jnp.broadcast_to(power, (1, LANES))
         high, low = halves(jnp.concatenate(parts, axis=0))
-        moved = dot(high, z_high) + (dot(low, z_high) + dot(high, z_low))
+        moved = dot(jnp.concatenate([high, low], axis=1), z_both) + dot(high, z_low)
         columns = []
         for t in range(2):
             real = moved[2 * t * rows : (2 * t + 1) * rows]
@@ -173,59 +179,60 @@
 
     half = blocks // 2
     left = lane[:COUNT] < points
+    depth = lax.broadcasted_iota(jnp.int32, (SLAB * points, LANES), 0)
+    scale = jnp.exp2(-powers[...])
+    last = tiles * COUNT
+    for target in range(out.shape[0]):
+        out[target, last : last + COUNT] = powers[...]
 
     def one_pair(k, carry):
-        picked = []
+        sources = ([], [])
         for part in range(2):
-            for y in range(SLAB):
-                for x in range(SLAB):
+            for x in range(SLAB):
+                lines = []
+                for y in range(SLAB):
                     start = (k * SLAB + y) * SLAB + x
-                    picked.append(field[part, pl.ds(start, COUNT, stride=rows), :])
-        high, low = halves(jnp.concatenate(picked, axis=0))
-        source = jnp.concatenate([high, low], axis=1)
-        chosen = []
-        for side in range(2):
-            row = (k + half * side) * tiles
-            index = [grid[pl.ds(row + j, 1), :] for j in range(tiles)]
-            depth = lax.broadcasted_iota(jnp.int32, (points, LANES), 0)
-            match = jnp.concatenate(
-                [jnp.where((i & (points - 1)) == depth, 1.0, 0.0) for i in index], axis=1
-            ).astype(jnp.bfloat16)
-            empty = jnp.zeros_like(match)
-            order = [match, empty] if side == 0 else [empty, match]
-            chosen.append(jnp.concatenate(order + order, axis=0))
-        values = dot(source, jnp.concatenate(chosen, axis=1))
+                    lines.append(field[part, pl.ds(start, COUNT, stride=rows), :])
+                turned = [pltpu.roll(line, points, 1) for line in lines]
+                sources[0].append(
+                    jnp.concatenate(
+                        [jnp.where(left, lines[y], turned[y + 1]) for y in range(0, SLAB, 2)], axis=1
+                    )
+                )
+                sources[1].append(
+                    jnp.concatenate(
+                        [jnp.where(left, turned[y], lines[y + 1]) for y in range(0, SLAB, 2)], axis=1
+                    )
+                )
         for side in range(2):
             block = k + half * side
+            high, low = halves(jnp.concatenate(sources[side], axis=0))
+            match = []
+            for j in range(tiles):
+                index = grid[pl.ds(block * tiles + j, 1), :] & (SLAB * points - 1)
+                match.append(jnp.where(index == depth, 1.0, 0.0).astype(jnp.bfloat16))
+            match = jnp.concatenate(match, axis=1)
+            values = dot(jnp.concatenate([high, low], axis=0), match)
+            count = 2 * SLAB * COUNT
+            values = values[:count] + values[count:]
             for j in range(tiles):
                 row = block * tiles + j
-                at = (side * tiles + j) * LANES
-                index = jnp.broadcast_to(grid[pl.ds(row, 1), :], (COUNT, LANES))
-                wave_y = (index // points) & (SLAB - 1)
+                at = slice(j * LANES, (j + 1) * LANES)
                 total_real = jnp.zeros((COUNT, LANES), jnp.float32)
                 total_imag = jnp.zeros((COUNT, LANES), jnp.float32)
                 for x in range(SLAB):
-                    pieces = []
-                    for part in range(2):
-                        of = [
-                            values[((part * SLAB + y) * SLAB + x) * COUNT :][:COUNT, at : at + LANES]
-                            for y in range(SLAB)
-                        ]
-                        pieces.append(
-                            jnp.where(
-                                wave_y < 2,
-                                jnp.where(wave_y == 0, of[0], of[1]),
-                                jnp.where(wave_y == 2, of[2], of[3]),
-                            )
-                        )
+                    real = values[x * COUNT : (x + 1) * COUNT, at]
+                    imag = values[(SLAB + x) * COUNT : (SLAB + x + 1) * COUNT, at]
                     cosine = waves[2 * x, pl.ds(row, 1), :]
                     sine = waves[2 * x + 1, pl.ds(row, 1), :]
-                    total_real += pieces[0] * cosine + pieces[1] * sine
-                    total_imag += pieces[1] * cosine - pieces[0] * sine
-                low = jnp.where(left, total_real, pltpu.roll(total_imag, points, 1))
-                high = jnp.where(left, pltpu.roll(total_real, points, 1), total_imag)
-                out[block, j * COUNT : (j + 1) * COUNT] = low
-                out[blocks + block, j * COUNT : (j + 1) * COUNT] = high
+                    total_real += real * cosine + imag * sine
+                    total_imag += imag * cosine - real * sine
+                total_real *= scale
+                total_imag *= scale
+                first = jnp.where(left, total_real, pltpu.roll(total_imag, points, 1))
+                second = jnp.where(left, pltpu.roll(total_real, points, 1), total_imag)
+                out[block, j * COUNT : (j + 1) * COUNT] = first
+                out[blocks + block, j * COUNT : (j + 1) * COUNT] = second
         return carry
 
     lax.fori_loop(0, half, one_pair, 0)
@@ -236,23 +243,25 @@
     lane = lax.broadcasted_iota(jnp.int32, (COUNT, LANES), 1)
     own = jnp.where(lane < LANES // 2, 0, 1) == (side[0] & 1)
     factors = []
-    for j in range(partial.shape[1] // COUNT):
+    last = partial.shape[1] - COUNT
+    for j in range(last // COUNT):
         root = jnp.sqrt(coulomb[:, j * LANES : (j + 1) * LANES])
         root = jnp.broadcast_to(root, (COUNT, LANES))
         factors.append(jnp.where(own, root, pltpu.roll(root, LANES // 2, 1)))
     factor = jnp.concatenate(factors, axis=0)
     pieces = []
     for first in (0, half):
-        total = partial[first]
-        for source in range(first + 1, first + half):
-            total += partial[source]
+        total = jnp.zeros((last, LANES), jnp.float32)
+        for source in range(first, first + half):
+            power = jnp.exp2(partial[source, last:])
+            total += partial[source, :last] * jnp.concatenate([power] * (last // COUNT), axis=0)
         pieces.append((total * scale) * factor)
     weighted = jnp.concatenate(pieces, axis=0).astype(jnp.bfloat16)
     for target in range(out.shape[0]):
         out[target] = weighted
 
 
-def panel_kernel(width, position, line_index, chip, gathered, out):
+def panel_kernel(width, position, line_index, chip, gathered, out, terms):
     line, group = line_index[0], (chip[0] >> 1) ^ ((position[0] >> 1) & 1)
     senders, height = gathered.shape[0], gathered.shape[1] // 2
     tiles = height // COUNT
@@ -276,19 +285,27 @@
         (((1,), (1,)), ((), ())),
         preferred_element_type=jnp.float32,
     )
-    out[...] = jnp.zeros_like(out)
-    count = 4 * COUNT
-    slot = 0
+    span = terms.shape[2]
+    for tile in range(terms.shape[0]):
+        terms[tile] = total[:, tile * span : (tile + 1) * span]
+    slots = {}
     for far in range(2):
         for side in range(2):
-            start = (2 * far + side) * COUNT
-            real = total[start : start + COUNT]
-            imag = total[count + start : count + start + COUNT]
             for column in last_columns(out.shape[0] // 2, far):
-                at = slice(column * width, (column + 1) * width)
-                out[slot, :, :width] = real[:, at]
-                out[slot, :, LANES // 2 : LANES // 2 + width] = imag[:, at]
-                slot += 1
+                slots[column, 2 * far + side] = len(slots)
+    rows = [
+        [terms[tile, pl.ds(a, 2 * 4, stride=COUNT), :] for a in range(COUNT)]
+        for tile in range(terms.shape[0])
+    ]
+    for column in range(out.shape[0] // 2):
+        tile, start = divmod(column * width, span)
+        at = slice(start, start + width)
+        line = jnp.concatenate([row[:, at] for row in rows[tile]], axis=1)
+        for which in range(4):
+            if (column, which) in slots:
+                for part in range(2):
+                    at = 4 * part + which
+                    out[slots[column, which], part : part + 1] = line[at : at + 1]
 
 
 def sum_kernel(scale, partial, out):
@@ -297,8 +314,8 @@
         total += partial[source]
     total *= scale
     width = out.shape[2]
-    out[0] = total[:, :width]
-    out[1] = total[:, LANES // 2 : LANES // 2 + width]
+    for row in range(COUNT):
+        out[:, row] = total[:, row * width : (row + 1) * width]
 
 
 def last_columns(groups, far):
@@ -318,7 +335,8 @@
     tiles = per_device // LANES
     rows = points // 2 * SLAB
     height = tiles * COUNT
-    width = lines * chips * COUNT // groups
+    columns = lines * chips * COUNT
+    width, span = columns // groups, min(columns, LANES)
 
     def turned(array):
         lead = array.shape[:-2]
@@ -354,7 +372,7 @@
     along_z, along_y, twist = tables(points)
     partial = pl.pallas_call(
         functools.partial(transform_kernel, points),
-        out_shape=jax.ShapeDtypeStruct((2 * groups, height, LANES), jnp.float32),
+        out_shape=jax.ShapeDtypeStruct((2 * groups, height + COUNT, LANES), jnp.float32),
         in_specs=[smem] * 3 + [anywhere] * 7,
         out_specs=vmem,
         scratch_shapes=[
@@ -367,6 +385,7 @@
             pltpu.VMEM(twist.shape, jnp.float32),
             pltpu.VMEM((2, COUNT * rows, LANES), jnp.float32),
             pltpu.VMEM((2 * SLAB, groups * tiles, LANES), jnp.float32),
+            pltpu.VMEM((COUNT, LANES), jnp.float32),
             pltpu.SemaphoreType.DMA((5 + 2 * COUNT,)),
         ],
         compiler_params=pltpu.CompilerParams(vmem_limit_bytes=62 * 1024 * 1024),
@@ -383,7 +402,7 @@
         along_y,
         twist,
     )
-    partial = exchange(partial, ("tc", "ga"), by_planes)
+    partial = exchange(partial.astype(jnp.float16), ("tc", "ga"), by_planes).astype(jnp.float32)
     copies = pl.pallas_call(
         functools.partial(weight_kernel, float(points) ** -1.5),
         out_shape=jax.ShapeDtypeStruct((lines * chips // 2, 2 * height, LANES), jnp.bfloat16),
@@ -395,9 +414,10 @@
     gathered = exchange(copies, ("tr", "tc"), by_rows)
     terms = pl.pallas_call(
         functools.partial(panel_kernel, width),
-        out_shape=jax.ShapeDtypeStruct((2 * groups, COUNT, LANES), jnp.float32),
+        out_shape=jax.ShapeDtypeStruct((2 * groups, 2, COUNT * width), jnp.float32),
         in_specs=[smem] * 3 + [vmem],
         out_specs=vmem,
+        scratch_shapes=[pltpu.VMEM((columns // span, 2 * 4 * COUNT, span), jnp.float32)],
         compiler_params=limit,
         name="panel",
     )(position, line, chip, gathered)

time: 84.3 us -> 79.8 us (0.947)
  waiting for transfers between devices: 30.8 us -> 25.2 us
  other arithmetic: 0 us -> 2 us
  blocking collectives: 13.5 us -> 12.5 us
    all_to_all x2, waiting for transfers between devices: 30.8 us -> 25.2 us  [exchange(): lax.all_to_all(array, names, split_axis=0, concat_axis=0, tiled=True, axi...]
    convert_element_type x0 -> x2, other arithmetic: none -> 2 us  [the longest x1 1.95 us: body(): partial.astype(jnp.float16)]
    all_to_all x1, blocking collectives: 13.5 us -> 12.5 us  [exchange(): lax.all_to_all(array, names, split_axis=0, concat_axis=0, tiled=True, axi...]
where the time goes in v4:
time: 79.8 us; the launch traced here: 79.4 us
  starting transfers between devices  26.7 us (33%)
  waiting for transfers between devices  25.2 us (32%)
  blocking collectives  12.5 us (16%)
  Pallas kernels  12.2 us (15%)
  other arithmetic  2 us (3%)
    all_to_all x2, starting transfers between devices, exchange(): lax.all_to_all(array, names, split_axis=0, concat_axis=0, tiled=True, axi...  26.7 us
    all_to_all x2, waiting for transfers between devices, exchange(): lax.all_to_all(array, names, split_axis=0, concat_axis=0, tiled=True, axi...  25.2 us
    all_to_all x1, blocking collectives, exchange(): lax.all_to_all(array, names, split_axis=0, concat_axis=0, tiled=True, axi...  12.5 us
    pallas_call x1, Pallas kernels, body(): pl.pallas_call(functools.partial(transform_kernel, points), out_shape=jax...  10.2 us
    convert_element_type x1, other arithmetic, body(): partial.astype(jnp.float16)  1.95 us
  transfers between devices with their start and end apart: 2, of which 2 were waited for; matrix products, arithmetic and copies ran while one was open for 0% of the time, Pallas kernels for 0%

profile of v4, /device:TPU:1, one launch (start us, length us, event | category | flops | bytes accessed | tf_op | source)
XLA Modules:
  0.0 79.4 jit_solution(8716324533176893786)
XLA Ops:
  0.0 10.2 %transform.1 = f32[32,48,128]{2,1,0:T(8,128)} custom-call(s32[8]{0:T(128)} %valence_ids.1, s32[8]{0:T(128)} %conduct_ids.1, s32[1]{0:T(128)} %bitcast.position, bf16[2,16,128,128]{3,2,1,0:T(8,128)(2,1)} %bitcast.19, bf16[2,16,128,128]{3,2,1,0:T(8,128)(2,1)} %bitcast.20, bf16[2,128,128]{2,1,0:T(8,128)(2,1)} %bitcast.21, s32[80,128]{1,0:T(8,128)} %bitcast.22, ...), custom_call_target="tpu_custom_call" | custom-call | tf_op jit(solution)/shard_map/transform/pallas_call | solution.py:373
  10.2 1.9 %convert_element_type.6 = f16[32,48,128]{2,1,0:T(8,128)(2,1)} convert(f32[32,48,128]{2,1,0:T(8,128)} %transform.1) | non-fusion elementwise | flops 196608 | bytes 1179648 | tf_op jit(solution)/shard_map/convert_element_type | solution.py:405
  12.2 14.4 %all-to-all-start = ((f16[32,48,128]{2,1,0:T(8,128)(2,1)}), f16[32,48,128]{2,1,0:T(8,128)(2,1)S(1)}, u32[]{:S(2)}, u32[]{:S(2)}) async-start(f16[32,48,128]{2,1,0:T(8,128)(2,1)} %convert_element_type.6), calls=%async_computation | async-start | bytes 786432 | tf_op jit(solution)/shard_map/all_to_all | solution.py:326
  26.6 0.0 copy-start
  26.6 0.7 copy-done
  27.3 12.0 %all-to-all-done = f16[32,48,128]{2,1,0:T(8,128)(2,1)S(1)} async-done(((f16[32,48,128]{2,1,0:T(8,128)(2,1)}), f16[32,48,128]{2,1,0:T(8,128)(2,1)S(1)}, u32[]{:S(2)}, u32[]{:S(2)}) %all-to-all-start) | async-done | bytes 393248 | tf_op jit(solution)/shard_map/all_to_all | solution.py:326
  39.3 0.1 convert_element_type.7.partial
  39.4 0.8 %weight.1 = bf16[16,80,128]{2,1,0:T(8,128)(2,1)} custom-call(s32[1]{0:T(128)} %bitcast.2.side.chip, f32[32,48,128]{2,1,0:T(8,128)S(1)} %convert_element_type.7.partial, f32[1,640]{1,0:T(1,128)S(1)} %reshape.43.coulomb), custom_call_target="tpu_custom_call" | custom-call | tf_op jit(solution)/shard_map/weight/pallas_call | solution.py:406
  40.2 12.3 %all-to-all-start.1 = ((bf16[16,80,128]{2,1,0:T(8,128)(2,1)}), bf16[16,80,128]{2,1,0:T(8,128)(2,1)S(1)}, u32[]{:S(2)}, u32[]{:S(2)}) async-start(bf16[16,80,128]{2,1,0:T(8,128)(2,1)} %weight.1), calls=%async_computation.1 | async-start | bytes 655360 | tf_op jit(solution)/shard_map/all_to_all | solution.py:326
  52.5 13.2 %all-to-all-done.1.gathered = bf16[16,80,128]{2,1,0:T(8,128)(2,1)S(1)} async-done(((bf16[16,80,128]{2,1,0:T(8,128)(2,1)}), bf16[16,80,128]{2,1,0:T(8,128)(2,1)S(1)}, u32[]{:S(2)}, u32[]{:S(2)}) %all-to-all-start.1) | async-done | bytes 327712 | tf_op jit(solution)/shard_map/all_to_all | solution.py:326
  65.7 0.4 panel.1
  66.1 12.5 %all_to_all.15.partial = f32[32,2,128]{2,1,0:T(2,128)S(1)} all-to-all(f32[32,2,128]{2,1,0:T(2,128)S(1)} %panel.1), channel_id=1, replica_groups={{0,1,4,5,8,9,12,13,16,17,20,21,24,25,28,29,34,35,38,39,42,43,46,47,50,5..., dimensions={0} | all-to-all | bytes 65536 | tf_op jit(solution)/shard_map/all_to_all | solution.py:326
  78.6 0.7 total.1
  (1 shorter events, 0.0 us)
Async XLA Ops:
  12.2 27.1 %all-to-all-start = ((f16[32,48,128]{2,1,0:T(8,128)(2,1)}), f16[32,48,128]{2,1,0:T(8,128)(2,1)S(1)}, u32[]{:S(2)}, u32[]{:S(2)}) async-start(f16[32,48,128]{2,1,0:T(8,128)(2,1)} %convert_element_type.6), calls=%async_computation | async-start | bytes 786432 | tf_op jit(solution)/shard_map/all_to_all | solution.py:326
  26.6 0.7 copy-start
  40.2 25.5 %all-to-all-start.1 = ((bf16[16,80,128]{2,1,0:T(8,128)(2,1)}), bf16[16,80,128]{2,1,0:T(8,128)(2,1)S(1)}, u32[]{:S(2)}, u32[]{:S(2)}) async-start(bf16[16,80,128]{2,1,0:T(8,128)(2,1)} %weight.1), calls=%async_computation.1 | async-start | bytes 655360 | tf_op jit(solution)/shard_map/all_to_all | solution.py:326

commit v5 on v4

--- a/solution.py
+++ b/solution.py
@@ -141,10 +141,12 @@
     lane = lax.broadcasted_iota(jnp.int32, (rows, LANES), 1)
     sign = jnp.where(lane < points, 1.0, -1.0).astype(jnp.float32)
     for first in range(0, COUNT, 2):
+        if first % 4 == 0:
+            for pair in bands[first : first + 4]:
+                for copy in pair:
+                    copy.wait()
         parts = []
         for t in (first, first + 1):
-            for copy in bands[t]:
-                copy.wait()
             left_real = left_rows[t, 0].astype(jnp.float32)
             left_imag = left_rows[t, 1].astype(jnp.float32)
             right_real = right_rows[t, 0].astype(jnp.float32) + common_real
@@ -235,13 +237,13 @@
                 out[blocks + block, j * COUNT : (j + 1) * COUNT] = second
         return carry
 
-    lax.fori_loop(0, half, one_pair, 0)
+    lax.fori_loop(0, half, one_pair, 0, unroll=4)
 
 
 def weight_kernel(scale, side, partial, coulomb, out):
     half = partial.shape[0] // 2
     lane = lax.broadcasted_iota(jnp.int32, (COUNT, LANES), 1)
-    own = jnp.where(lane < LANES // 2, 0, 1) == (side[0] & 1)
+    own = jnp.where(lane < LANES // 2, 0, 1) == (side[0] >> 1)
     factors = []
     last = partial.shape[1] - COUNT
     for j in range(last // COUNT):
@@ -262,7 +264,8 @@
 
 
 def panel_kernel(width, position, line_index, chip, gathered, out, terms):
-    line, group = line_index[0], (chip[0] >> 1) ^ ((position[0] >> 1) & 1)
+    line = line_index[0]
+    parity = ((chip[0] >> 1) ^ chip[0] ^ (position[0] >> 1)) & 1
     senders, height = gathered.shape[0], gathered.shape[1] // 2
     tiles = height // COUNT
     lane = lax.broadcasted_iota(jnp.int32, (1, LANES), 1)
@@ -271,12 +274,18 @@
     def by_tile(array):
         shape = array.shape[:-2] + (2, tiles, COUNT, LANES)
         array = array.astype(jnp.float32).reshape(shape)
-        return [array[..., j, :, :].reshape(-1, LANES) for j in range(tiles)]
-
-    right = [tile.astype(jnp.bfloat16) for tile in by_tile(gathered[...])]
-    rows = jnp.stack([gathered[2 * line + group], gathered[2 * line + 1 - group]])
+        return [array[..., j, :, :] for j in range(tiles)]
+
+    right = []
+    for tile in by_tile(gathered[...]):
+        order = [tile[2 * i + low, high] for i in range(senders // 2) for high in range(2) for low in range(2)]
+        right.append(jnp.concatenate(order, axis=0).astype(jnp.bfloat16))
+    near = by_tile(gathered[2 * line + parity])
+    away = by_tile(gathered[2 * line + 1 - parity])
     left = []
-    for tile in by_tile(rows):
+    for j in range(tiles):
+        order = [(near, away)[far ^ high][j][high] for far in range(2) for high in range(2)]
+        tile = jnp.concatenate(order, axis=0)
         turned = pltpu.roll(tile, LANES // 2, 1) * sign
         left.append(jnp.concatenate([tile, turned], axis=0).astype(jnp.bfloat16))
     total = lax.dot_general(
@@ -352,21 +361,20 @@
     limit = pltpu.CompilerParams(vmem_limit_bytes=16 * 1024 * 1024)
 
     by_planes = [
-        [(2 * high + low) * groups + g for low in range(2) for g in range(groups)]
-        for high in range(chips // 2)
+        [(2 * high + low) * groups + g for high in range(2) for g in range(groups)]
+        for low in range(2)
     ]
     by_rows = [
-        [i * chips + 2 * high + low for i in range(lines) for high in range(chips // 2)]
-        for low in range(2)
+        [i * chips + 2 * high + low for i in range(lines) for low in range(2)] for high in range(2)
     ]
     by_columns = [
         [
-            (2 * (high ^ far) + low) * groups + g
+            (2 * high + (far ^ high ^ parity)) * groups + g
             for far in range(2)
-            for low in range(2)
+            for high in range(2)
             for g in last_columns(groups, far)
         ]
-        for high in range(chips // 2)
+        for parity in range(2)
     ]
 
     along_z, along_y, twist = tables(points)

time: 79.8 us -> 76.3 us (0.956)
  blocking collectives: 12.5 us -> 15 us
  starting transfers between devices: 26.7 us -> 24.4 us
  Pallas kernels: 12.2 us -> 10.1 us
  waiting for transfers between devices: 25.2 us -> 23.6 us
    all_to_all x1, blocking collectives: 12.5 us -> 15 us  [exchange(): lax.all_to_all(array, names, split_axis=0, concat_axis=0, tiled=True, axi...]
    all_to_all x2, starting transfers between devices: 26.7 us -> 24.4 us  [exchange(): lax.all_to_all(array, names, split_axis=0, concat_axis=0, tiled=True, axi...]
    pallas_call x1, Pallas kernels: 10.2 us -> 8.18 us  [body(): pl.pallas_call(functools.partial(transform_kernel, points), out_shape=jax...]
    all_to_all x2, waiting for transfers between devices: 25.2 us -> 23.6 us  [exchange(): lax.all_to_all(array, names, split_axis=0, concat_axis=0, tiled=True, axi...]
where the time goes in v5:
time: 76.3 us; the launch traced here: 75.9 us
  starting transfers between devices  24.4 us (32%)
  waiting for transfers between devices  23.6 us (31%)
  blocking collectives  15 us (20%)
  Pallas kernels  10.1 us (13%)
  other arithmetic  2 us (3%)
    all_to_all x2, starting transfers between devices, exchange(): lax.all_to_all(array, names, split_axis=0, concat_axis=0, tiled=True, axi...  24.4 us
    all_to_all x2, waiting for transfers between devices, exchange(): lax.all_to_all(array, names, split_axis=0, concat_axis=0, tiled=True, axi...  23.6 us
    all_to_all x1, blocking collectives, exchange(): lax.all_to_all(array, names, split_axis=0, concat_axis=0, tiled=True, axi...  15 us
    pallas_call x1, Pallas kernels, body(): pl.pallas_call(functools.partial(transform_kernel, points), out_shape=jax...  8.18 us
    convert_element_type x1, other arithmetic, body(): partial.astype(jnp.float16)  1.95 us
  transfers between devices with their start and end apart: 2, of which 2 were waited for; matrix products, arithmetic and copies ran while one was open for 0% of the time, Pallas kernels for 0%

profile of v5, /device:TPU:1, one launch (start us, length us, event | category | flops | bytes accessed | tf_op | source)
XLA Modules:
  0.0 75.9 jit_solution(10888061433035450311)
XLA Ops:
  0.0 8.2 %transform.1 = f32[32,48,128]{2,1,0:T(8,128)} custom-call(s32[8]{0:T(128)} %valence_ids.1, s32[8]{0:T(128)} %conduct_ids.1, s32[1]{0:T(128)} %bitcast.position, bf16[2,16,128,128]{3,2,1,0:T(8,128)(2,1)} %bitcast.19, bf16[2,16,128,128]{3,2,1,0:T(8,128)(2,1)} %bitcast.20, bf16[2,128,128]{2,1,0:T(8,128)(2,1)} %bitcast.21, s32[80,128]{1,0:T(8,128)} %bitcast.22, ...), custom_call_target="tpu_custom_call" | custom-call | tf_op jit(solution)/shard_map/transform/pallas_call | solution.py:381
  8.2 1.9 %convert_element_type.6 = f16[32,48,128]{2,1,0:T(8,128)(2,1)} convert(f32[32,48,128]{2,1,0:T(8,128)} %transform.1) | non-fusion elementwise | flops 196608 | bytes 1179648 | tf_op jit(solution)/shard_map/convert_element_type | solution.py:413
  10.1 14.4 %all-to-all-start = ((f16[32,48,128]{2,1,0:T(8,128)(2,1)}), f16[32,48,128]{2,1,0:T(8,128)(2,1)S(1)}, u32[]{:S(2)}, u32[]{:S(2)}) async-start(f16[32,48,128]{2,1,0:T(8,128)(2,1)} %convert_element_type.6), calls=%async_computation | async-start | bytes 786432 | tf_op jit(solution)/shard_map/all_to_all | solution.py:335
  24.6 0.0 copy-start
  24.6 0.7 copy-done
  25.3 12.7 %all-to-all-done = f16[32,48,128]{2,1,0:T(8,128)(2,1)S(1)} async-done(((f16[32,48,128]{2,1,0:T(8,128)(2,1)}), f16[32,48,128]{2,1,0:T(8,128)(2,1)S(1)}, u32[]{:S(2)}, u32[]{:S(2)}) %all-to-all-start) | async-done | bytes 393248 | tf_op jit(solution)/shard_map/all_to_all | solution.py:335
  37.9 0.1 convert_element_type.7.partial
  38.0 0.8 %weight.1 = bf16[16,80,128]{2,1,0:T(8,128)(2,1)} custom-call(s32[1]{0:T(128)} %bitcast.2.side.chip, f32[32,48,128]{2,1,0:T(8,128)S(1)} %convert_element_type.7.partial, f32[1,640]{1,0:T(1,128)S(1)} %reshape.43.coulomb), custom_call_target="tpu_custom_call" | custom-call | tf_op jit(solution)/shard_map/weight/pallas_call | solution.py:414
  38.8 10.0 %all-to-all-start.1 = ((bf16[16,80,128]{2,1,0:T(8,128)(2,1)}), bf16[16,80,128]{2,1,0:T(8,128)(2,1)S(1)}, u32[]{:S(2)}, u32[]{:S(2)}) async-start(bf16[16,80,128]{2,1,0:T(8,128)(2,1)} %weight.1), calls=%async_computation.1 | async-start | bytes 655360 | tf_op jit(solution)/shard_map/all_to_all | solution.py:335
  48.8 10.9 %all-to-all-done.1.gathered = bf16[16,80,128]{2,1,0:T(8,128)(2,1)S(1)} async-done(((bf16[16,80,128]{2,1,0:T(8,128)(2,1)}), bf16[16,80,128]{2,1,0:T(8,128)(2,1)S(1)}, u32[]{:S(2)}, u32[]{:S(2)}) %all-to-all-start.1) | async-done | bytes 327712 | tf_op jit(solution)/shard_map/all_to_all | solution.py:335
  59.7 0.4 panel.1
  60.1 15.0 %all_to_all.15.partial = f32[32,2,128]{2,1,0:T(2,128)S(1)} all-to-all(f32[32,2,128]{2,1,0:T(2,128)S(1)} %panel.1), channel_id=1, replica_groups={{0,1,4,5,8,9,12,13,48,49,52,53,56,57,60,61,18,19,22,23,26,27,30,31,34,3..., dimensions={0} | all-to-all | bytes 65536 | tf_op jit(solution)/shard_map/all_to_all | solution.py:335
  75.1 0.7 total.1
  (1 shorter events, 0.0 us)
Async XLA Ops:
  10.1 27.8 %all-to-all-start = ((f16[32,48,128]{2,1,0:T(8,128)(2,1)}), f16[32,48,128]{2,1,0:T(8,128)(2,1)S(1)}, u32[]{:S(2)}, u32[]{:S(2)}) async-start(f16[32,48,128]{2,1,0:T(8,128)(2,1)} %convert_element_type.6), calls=%async_computation | async-start | bytes 786432 | tf_op jit(solution)/shard_map/all_to_all | solution.py:335
  24.6 0.7 copy-start
  38.8 20.9 %all-to-all-start.1 = ((bf16[16,80,128]{2,1,0:T(8,128)(2,1)}), bf16[16,80,128]{2,1,0:T(8,128)(2,1)S(1)}, u32[]{:S(2)}, u32[]{:S(2)}) async-start(bf16[16,80,128]{2,1,0:T(8,128)(2,1)} %weight.1), calls=%async_computation.1 | async-start | bytes 655360 | tf_op jit(solution)/shard_map/all_to_all | solution.py:335

commit v6 on v5

--- a/solution.py
+++ b/solution.py
@@ -69,7 +69,6 @@
     points,
     valence_ids,
     conduct_ids,
-    position,
     valence,
     conduction,
     envelope,
@@ -77,7 +76,7 @@
     along_z_source,
     along_y_source,
     twist_source,
-    out,
+    result,
     left_rows,
     right_rows,
     common,
@@ -88,10 +87,12 @@
     field,
     waves,
     powers,
+    out,
     arrived,
+    sent,
 ):
     rows = points // 2 * SLAB
-    blocks = out.shape[0] // 2
+    blocks = result.shape[0] // 2
     tiles = grid.shape[0] // blocks
     dot = functools.partial(jnp.dot, preferred_element_type=jnp.float32)
 
@@ -103,35 +104,30 @@
         copies.append(copy)
         return copy
 
-    whole = [
+    for source, target in (
+        (grid_source, grid),
+        (along_z_source, along_z),
+        (envelope, common),
+        (along_y_source, along_y),
+        (twist_source, twist),
+    ):
         fetch(source, target)
-        for source, target in (
-            (grid_source, grid),
-            (along_z_source, along_z),
-            (envelope, common),
-            (along_y_source, along_y),
-            (twist_source, twist),
-        )
-    ]
-    bands = []
     for t in range(COUNT):
-        bands.append(
-            (
-                fetch(valence.at[:, valence_ids[t]], left_rows.at[t]),
-                fetch(conduction.at[:, conduct_ids[t]], right_rows.at[t]),
-            )
-        )
-    whole[0].wait()
-
+        fetch(valence.at[:, valence_ids[t]], left_rows.at[t])
+        fetch(conduction.at[:, conduct_ids[t]], right_rows.at[t])
+    copies[0].wait()
+
+    position = lax.axis_index("ga")
     wave_x = grid[...] // (points * points)
     for plane in range(SLAB):
-        steps = ((position[0] * SLAB + plane) * wave_x) & (points - 1)
+        steps = ((position * SLAB + plane) * wave_x) & (points - 1)
         cosine, sine = unit_circle(steps, points)
         waves[2 * plane] = cosine
         waves[2 * plane + 1] = sine
 
-    for copy in whole[1:]:
+    for copy in copies[1:]:
         copy.wait()
+
     z_high, z_low = halves(along_z[...])
     z_both = jnp.concatenate([z_high, z_high], axis=0)
     y_high, y_low = halves(along_y[...])
@@ -141,10 +137,6 @@
     lane = lax.broadcasted_iota(jnp.int32, (rows, LANES), 1)
     sign = jnp.where(lane < points, 1.0, -1.0).astype(jnp.float32)
     for first in range(0, COUNT, 2):
-        if first % 4 == 0:
-            for pair in bands[first : first + 4]:
-                for copy in pair:
-                    copy.wait()
         parts = []
         for t in (first, first + 1):
             left_real = left_rows[t, 0].astype(jnp.float32)
@@ -184,10 +176,11 @@
     depth = lax.broadcasted_iota(jnp.int32, (SLAB * points, LANES), 0)
     scale = jnp.exp2(-powers[...])
     last = tiles * COUNT
-    for target in range(out.shape[0]):
-        out[target, last : last + COUNT] = powers[...]
-
-    def one_pair(k, carry):
+    for slot in range(out.shape[0]):
+        out[slot, last : last + COUNT] = powers[...]
+
+    copies = []
+    for k in range(half):
         sources = ([], [])
         for part in range(2):
             for x in range(SLAB):
@@ -235,20 +228,22 @@
                 second = jnp.where(left, pltpu.roll(total_real, points, 1), total_imag)
                 out[block, j * COUNT : (j + 1) * COUNT] = first
                 out[blocks + block, j * COUNT : (j + 1) * COUNT] = second
-        return carry
-
-    lax.fori_loop(0, half, one_pair, 0, unroll=4)
-
-
-def weight_kernel(scale, side, partial, coulomb, out):
+            for slot in (block, blocks + block):
+                copy = pltpu.make_async_copy(out.at[slot], result.at[slot], sent.at[slot])
+                copy.start()
+                copies.append(copy)
+    for copy in copies:
+        copy.wait()
+
+
+def weight_kernel(scale, partial, coulomb, out):
     half = partial.shape[0] // 2
+    last = partial.shape[1] - COUNT
     lane = lax.broadcasted_iota(jnp.int32, (COUNT, LANES), 1)
-    own = jnp.where(lane < LANES // 2, 0, 1) == (side[0] >> 1)
+    own = jnp.where(lane < LANES // 2, 0, 1) == lax.axis_index("tc") // 2
     factors = []
-    last = partial.shape[1] - COUNT
     for j in range(last // COUNT):
-        root = jnp.sqrt(coulomb[:, j * LANES : (j + 1) * LANES])
-        root = jnp.broadcast_to(root, (COUNT, LANES))
+        root = jnp.broadcast_to(jnp.sqrt(coulomb[j : j + 1]), (COUNT, LANES))
         factors.append(jnp.where(own, root, pltpu.roll(root, LANES // 2, 1)))
     factor = jnp.concatenate(factors, axis=0)
     pieces = []
@@ -263,9 +258,9 @@
         out[target] = weighted
 
 
-def panel_kernel(width, position, line_index, chip, gathered, out, terms):
-    line = line_index[0]
-    parity = ((chip[0] >> 1) ^ chip[0] ^ (position[0] >> 1)) & 1
+def panel_kernel(width, gathered, out, terms):
+    line, chip = lax.axis_index("tr"), lax.axis_index("tc")
+    parity = (chip // 2 + chip + lax.axis_index("ga") // 2) % 2
     senders, height = gathered.shape[0], gathered.shape[1] // 2
     tiles = height // COUNT
     lane = lax.broadcasted_iota(jnp.int32, (1, LANES), 1)
@@ -352,12 +347,9 @@
         split = array.reshape(lead + (SLAB, points // 2, LANES))
         return jnp.swapaxes(split, -3, -2).reshape(lead + (rows, LANES))
 
-    position, line, chip = (
-        lax.axis_index(name).astype(jnp.int32).reshape(1) for name in ("ga", "tr", "tc")
-    )
     smem = pl.BlockSpec(memory_space=pltpu.SMEM)
     vmem = pl.BlockSpec(memory_space=pltpu.VMEM)
-    anywhere = pl.BlockSpec(memory_space=pl.ANY)
+    hbm = pl.BlockSpec(memory_space=pl.ANY)
     limit = pltpu.CompilerParams(vmem_limit_bytes=16 * 1024 * 1024)
 
     by_planes = [
@@ -381,8 +373,8 @@
     partial = pl.pallas_call(
         functools.partial(transform_kernel, points),
         out_shape=jax.ShapeDtypeStruct((2 * groups, height + COUNT, LANES), jnp.float32),
-        in_specs=[smem] * 3 + [anywhere] * 7,
-        out_specs=vmem,
+        in_specs=[smem] * 2 + [hbm] * 7,
+        out_specs=hbm,
         scratch_shapes=[
             pltpu.VMEM((COUNT, 2, rows, LANES), jnp.bfloat16),
             pltpu.VMEM((COUNT, 2, rows, LANES), jnp.bfloat16),
@@ -394,14 +386,15 @@
             pltpu.VMEM((2, COUNT * rows, LANES), jnp.float32),
             pltpu.VMEM((2 * SLAB, groups * tiles, LANES), jnp.float32),
             pltpu.VMEM((COUNT, LANES), jnp.float32),
+            pltpu.VMEM((2 * groups, height + COUNT, LANES), jnp.float32),
             pltpu.SemaphoreType.DMA((5 + 2 * COUNT,)),
+            pltpu.SemaphoreType.DMA((2 * groups,)),
         ],
-        compiler_params=pltpu.CompilerParams(vmem_limit_bytes=62 * 1024 * 1024),
+        compiler_params=pltpu.CompilerParams(vmem_limit_bytes=60 * 1024 * 1024),
         name="transform",
     )(
         valence_index,
         conduction_index,
-        position,
         turned(valence),
         turned(conduction),
         turned(envelope),
@@ -414,21 +407,21 @@
     copies = pl.pallas_call(
         functools.partial(weight_kernel, float(points) ** -1.5),
         out_shape=jax.ShapeDtypeStruct((lines * chips // 2, 2 * height, LANES), jnp.bfloat16),
-        in_specs=[smem, vmem, vmem],
+        in_specs=[vmem, vmem],
         out_specs=vmem,
         compiler_params=limit,
         name="weight",
-    )(chip, partial, coulomb.reshape(1, per_device))
+    )(partial, coulomb.reshape(tiles, LANES))
     gathered = exchange(copies, ("tr", "tc"), by_rows)
     terms = pl.pallas_call(
         functools.partial(panel_kernel, width),
         out_shape=jax.ShapeDtypeStruct((2 * groups, 2, COUNT * width), jnp.float32),
-        in_specs=[smem] * 3 + [vmem],
+        in_specs=[vmem],
         out_specs=vmem,
         scratch_shapes=[pltpu.VMEM((columns // span, 2 * 4 * COUNT, span), jnp.float32)],
         compiler_params=limit,
         name="panel",
-    )(position, line, chip, gathered)
+    )(gathered)
     terms = exchange(terms, ("tc", "ga"), by_columns)
     return pl.pallas_call(
         functools.partial(sum_kernel, 1.0 / (per_device * groups)),

time: 76.3 us -> 74.9 us (0.982)
  blocking collectives: 15 us -> 63.3 us
  starting transfers between devices: 24.4 us -> 0 us
  waiting for transfers between devices: 23.6 us -> 0 us
    all_to_all x1 -> x3, blocking collectives: 15 us -> 63.3 us  [exchange(): lax.all_to_all(array, names, split_axis=0, concat_axis=0, tiled=True, axi...]
    all_to_all x2 -> x0, starting transfers between devices: 24.4 us -> none  [exchange(): lax.all_to_all(array, names, split_axis=0, concat_axis=0, tiled=True, axi...]
    all_to_all x2 -> x0, waiting for transfers between devices: 23.6 us -> none  [exchange(): lax.all_to_all(array, names, split_axis=0, concat_axis=0, tiled=True, axi...]
  transfers between devices with their start and end apart: 2 -> 0, of which waited for: 2 -> 0; matrix products, arithmetic and copies ran while one was open for 0% -> 0% of each run, Pallas kernels for 0% -> 0%
where the time goes in v6:
time: 74.9 us; the launch traced here: 74.6 us
  blocking collectives  63.3 us (85%)
  Pallas kernels  9.37 us (13%)
  other arithmetic  1.24 us (2%)
    all_to_all x3, blocking collectives, exchange(): lax.all_to_all(array, names, split_axis=0, concat_axis=0, tiled=True, axi...  63.3 us
    pallas_call x1, Pallas kernels, body(): pl.pallas_call(functools.partial(transform_kernel, points), out_shape=jax...  8.11 us

profile of v6, /device:TPU:1, one launch (start us, length us, event | category | flops | bytes accessed | tf_op | source)
XLA Modules:
  0.0 74.6 jit_solution(1296205589756290900)
XLA Ops:
  0.0 8.1 %transform.1 = f32[32,48,128]{2,1,0:T(8,128)} custom-call(s32[8]{0:T(128)} %valence_ids.1, s32[8]{0:T(128)} %conduct_ids.1, bf16[2,16,128,128]{3,2,1,0:T(8,128)(2,1)} %bitcast.18, bf16[2,16,128,128]{3,2,1,0:T(8,128)(2,1)} %bitcast.19, bf16[2,128,128]{2,1,0:T(8,128)(2,1)} %bitcast.20, s32[80,128]{1,0:T(8,128)} %bitcast.21, ...), custom_call_target="tpu_custom_call" | custom-call | tf_op jit(solution)/shard_map/transform/pallas_call | solution.py:373
  8.1 1.2 %convert_element_type.6 = f16[32,48,128]{2,1,0:T(8,128)(2,1)S(1)} convert(f32[32,48,128]{2,1,0:T(8,128)} %transform.1) | non-fusion elementwise | flops 196608 | bytes 1179648 | tf_op jit(solution)/shard_map/convert_element_type | solution.py:406
  9.3 27.6 %all_to_all.15 = f16[32,48,128]{2,1,0:T(8,128)(2,1)S(1)} all-to-all(f16[32,48,128]{2,1,0:T(8,128)(2,1)S(1)} %convert_element_type.6), channel_id=1, replica_groups={{0,1,2,3,4,5,6,7,8,9,10,11,12,13,14,15,32,33,34,35,36,37,38,39,40,41,42..., dimensions={0} | all-to-all | bytes 786432 | tf_op jit(solution)/shard_map/all_to_all | solution.py:330
  36.9 0.0 copy-start
  36.9 0.1 convert_element_type.7.partial
  37.0 0.6 copy-done
  37.6 0.1 weight.1
  37.7 20.7 %all_to_all.16.gathered = bf16[16,80,128]{2,1,0:T(8,128)(2,1)S(1)} all-to-all(bf16[16,80,128]{2,1,0:T(8,128)(2,1)S(1)} %weight.1), channel_id=1, replica_groups={{0,16,64,80,128,144,192,208,256,272,320,336,384,400,448,464},{32,48,96,..., dimensions={0} | all-to-all | bytes 655360 | tf_op jit(solution)/shard_map/all_to_all | solution.py:330
  58.4 0.4 panel.1
  58.8 15.0 %all_to_all.17.partial = f32[32,2,128]{2,1,0:T(2,128)S(1)} all-to-all(f32[32,2,128]{2,1,0:T(2,128)S(1)} %panel.1), channel_id=1, replica_groups={{0,1,4,5,8,9,12,13,48,49,52,53,56,57,60,61,18,19,22,23,26,27,30,31,34,3..., dimensions={0} | all-to-all | bytes 65536 | tf_op jit(solution)/shard_map/all_to_all | solution.py:330
  73.8 0.7 total.1
Async XLA Ops:
  36.9 0.7 copy-start

commit v7 on v6

--- a/solution.py
+++ b/solution.py
@@ -173,7 +173,8 @@
 
     half = blocks // 2
     left = lane[:COUNT] < points
-    depth = lax.broadcasted_iota(jnp.int32, (SLAB * points, LANES), 0)
+    depth = lax.broadcasted_iota(jnp.int32, (SLAB * points, LANES), 0).astype(jnp.bfloat16)
+    one, zero = (jnp.full(depth.shape, value, jnp.bfloat16) for value in (1.0, 0.0))
     scale = jnp.exp2(-powers[...])
     last = tiles * COUNT
     for slot in range(out.shape[0]):
@@ -205,7 +206,8 @@
             match = []
             for j in range(tiles):
                 index = grid[pl.ds(block * tiles + j, 1), :] & (SLAB * points - 1)
-                match.append(jnp.where(index == depth, 1.0, 0.0).astype(jnp.bfloat16))
+                index = jnp.broadcast_to(index.astype(jnp.bfloat16), depth.shape)
+                match.append(jnp.where(index == depth, one, zero))
             match = jnp.concatenate(match, axis=1)
             values = dot(jnp.concatenate([high, low], axis=0), match)
             count = 2 * SLAB * COUNT

time: 74.9 us -> 74.7 us (level)
  no operation moved by 1% of the time
where the time goes in v7:
time: 74.7 us; the launch traced here: 74.3 us
  blocking collectives  63.3 us (85%)
  Pallas kernels  9.14 us (12%)
  other arithmetic  1.24 us (2%)
    all_to_all x3, blocking collectives, exchange(): lax.all_to_all(array, names, split_axis=0, concat_axis=0, tiled=True, axi...  63.3 us
    pallas_call x1, Pallas kernels, body(): pl.pallas_call(functools.partial(transform_kernel, points), out_shape=jax...  7.88 us

profile of v7, /device:TPU:1, one launch (start us, length us, event | category | flops | bytes accessed | tf_op | source)
XLA Modules:
  0.0 74.3 jit_solution(8828652640524022471)
XLA Ops:
  0.0 7.9 %transform.1 = f32[32,48,128]{2,1,0:T(8,128)} custom-call(s32[8]{0:T(128)} %valence_ids.1, s32[8]{0:T(128)} %conduct_ids.1, bf16[2,16,128,128]{3,2,1,0:T(8,128)(2,1)} %bitcast.18, bf16[2,16,128,128]{3,2,1,0:T(8,128)(2,1)} %bitcast.19, bf16[2,128,128]{2,1,0:T(8,128)(2,1)} %bitcast.20, s32[80,128]{1,0:T(8,128)} %bitcast.21, ...), custom_call_target="tpu_custom_call" | custom-call | tf_op jit(solution)/shard_map/transform/pallas_call | solution.py:375
  7.9 1.2 %convert_element_type.6 = f16[32,48,128]{2,1,0:T(8,128)(2,1)S(1)} convert(f32[32,48,128]{2,1,0:T(8,128)} %transform.1) | non-fusion elementwise | flops 196608 | bytes 1179648 | tf_op jit(solution)/shard_map/convert_element_type | solution.py:408
  9.1 27.6 %all_to_all.15 = f16[32,48,128]{2,1,0:T(8,128)(2,1)S(1)} all-to-all(f16[32,48,128]{2,1,0:T(8,128)(2,1)S(1)} %convert_element_type.6), channel_id=1, replica_groups={{0,1,2,3,4,5,6,7,8,9,10,11,12,13,14,15,32,33,34,35,36,37,38,39,40,41,42..., dimensions={0} | all-to-all | bytes 786432 | tf_op jit(solution)/shard_map/all_to_all | solution.py:332
  36.7 0.0 copy-start
  36.7 0.1 convert_element_type.7.partial
  36.7 0.6 copy-done
  37.4 0.1 weight.1
  37.5 20.7 %all_to_all.16.gathered = bf16[16,80,128]{2,1,0:T(8,128)(2,1)S(1)} all-to-all(bf16[16,80,128]{2,1,0:T(8,128)(2,1)S(1)} %weight.1), channel_id=1, replica_groups={{0,16,64,80,128,144,192,208,256,272,320,336,384,400,448,464},{32,48,96,..., dimensions={0} | all-to-all | bytes 655360 | tf_op jit(solution)/shard_map/all_to_all | solution.py:332
  58.2 0.4 panel.1
  58.6 15.0 %all_to_all.17.partial = f32[32,2,128]{2,1,0:T(2,128)S(1)} all-to-all(f32[32,2,128]{2,1,0:T(2,128)S(1)} %panel.1), channel_id=1, replica_groups={{0,1,4,5,8,9,12,13,48,49,52,53,56,57,60,61,18,19,22,23,26,27,30,31,34,3..., dimensions={0} | all-to-all | bytes 65536 | tf_op jit(solution)/shard_map/all_to_all | solution.py:332
  73.6 0.7 total.1
Async XLA Ops:
  36.7 0.7 copy-start

commit v8 on v7

--- a/solution.py
+++ b/solution.py
@@ -125,7 +125,7 @@
         waves[2 * plane] = cosine
         waves[2 * plane + 1] = sine
 
-    for copy in copies[1:]:
+    for copy in copies[1:5]:
         copy.wait()
 
     z_high, z_low = halves(along_z[...])
@@ -137,6 +137,8 @@
     lane = lax.broadcasted_iota(jnp.int32, (rows, LANES), 1)
     sign = jnp.where(lane < points, 1.0, -1.0).astype(jnp.float32)
     for first in range(0, COUNT, 2):
+        for copy in copies[5 + 2 * first : 9 + 2 * first]:
+            copy.wait()
         parts = []
         for t in (first, first + 1):
             left_real = left_rows[t, 0].astype(jnp.float32)

time: 74.7 us -> 75.1 us (level)
  no operation moved by 1% of the time
where the time goes in v8:
time: 75.1 us; the launch traced here: 74.8 us
  blocking collectives  63.3 us (84%)
  Pallas kernels  9.61 us (13%)
  other arithmetic  1.24 us (2%)
    all_to_all x3, blocking collectives, exchange(): lax.all_to_all(array, names, split_axis=0, concat_axis=0, tiled=True, axi...  63.3 us
    pallas_call x1, Pallas kernels, body(): pl.pallas_call(functools.partial(transform_kernel, points), out_shape=jax...  8.35 us

profile of v8, /device:TPU:1, one launch (start us, length us, event | category | flops | bytes accessed | tf_op | source)
XLA Modules:
  0.0 74.8 jit_solution(12066967740320264813)
XLA Ops:
  0.0 8.4 %transform.1 = f32[32,48,128]{2,1,0:T(8,128)} custom-call(s32[8]{0:T(128)} %valence_ids.1, s32[8]{0:T(128)} %conduct_ids.1, bf16[2,16,128,128]{3,2,1,0:T(8,128)(2,1)} %bitcast.18, bf16[2,16,128,128]{3,2,1,0:T(8,128)(2,1)} %bitcast.19, bf16[2,128,128]{2,1,0:T(8,128)(2,1)} %bitcast.20, s32[80,128]{1,0:T(8,128)} %bitcast.21, ...), custom_call_target="tpu_custom_call" | custom-call | tf_op jit(solution)/shard_map/transform/pallas_call | solution.py:377
  8.4 1.2 %convert_element_type.6 = f16[32,48,128]{2,1,0:T(8,128)(2,1)S(1)} convert(f32[32,48,128]{2,1,0:T(8,128)} %transform.1) | non-fusion elementwise | flops 196608 | bytes 1179648 | tf_op jit(solution)/shard_map/convert_element_type | solution.py:410
  9.6 27.6 %all_to_all.15 = f16[32,48,128]{2,1,0:T(8,128)(2,1)S(1)} all-to-all(f16[32,48,128]{2,1,0:T(8,128)(2,1)S(1)} %convert_element_type.6), channel_id=1, replica_groups={{0,1,2,3,4,5,6,7,8,9,10,11,12,13,14,15,32,33,34,35,36,37,38,39,40,41,42..., dimensions={0} | all-to-all | bytes 786432 | tf_op jit(solution)/shard_map/all_to_all | solution.py:334
  37.2 0.0 copy-start
  37.2 0.1 convert_element_type.7.partial
  37.2 0.6 copy-done
  37.8 0.1 weight.1
  38.0 20.7 %all_to_all.16.gathered = bf16[16,80,128]{2,1,0:T(8,128)(2,1)S(1)} all-to-all(bf16[16,80,128]{2,1,0:T(8,128)(2,1)S(1)} %weight.1), channel_id=1, replica_groups={{0,16,64,80,128,144,192,208,256,272,320,336,384,400,448,464},{32,48,96,..., dimensions={0} | all-to-all | bytes 655360 | tf_op jit(solution)/shard_map/all_to_all | solution.py:334
  58.6 0.4 panel.1
  59.1 15.0 %all_to_all.17.partial = f32[32,2,128]{2,1,0:T(2,128)S(1)} all-to-all(f32[32,2,128]{2,1,0:T(2,128)S(1)} %panel.1), channel_id=1, replica_groups={{0,1,4,5,8,9,12,13,48,49,52,53,56,57,60,61,18,19,22,23,26,27,30,31,34,3..., dimensions={0} | all-to-all | bytes 65536 | tf_op jit(solution)/shard_map/all_to_all | solution.py:334
  74.1 0.7 total.1
Async XLA Ops:
  37.2 0.7 copy-start

commit v9 on v7

--- a/solution.py
+++ b/solution.py
@@ -136,9 +136,9 @@
     common_imag = common[1].astype(jnp.float32)
     lane = lax.broadcasted_iota(jnp.int32, (rows, LANES), 1)
     sign = jnp.where(lane < points, 1.0, -1.0).astype(jnp.float32)
-    for first in range(0, COUNT, 2):
+    for first in range(0, COUNT, 4):
         parts = []
-        for t in (first, first + 1):
+        for t in range(first, first + 4):
             left_real = left_rows[t, 0].astype(jnp.float32)
             left_imag = left_rows[t, 1].astype(jnp.float32)
             right_real = right_rows[t, 0].astype(jnp.float32) + common_real
@@ -152,7 +152,7 @@
         high, low = halves(jnp.concatenate(parts, axis=0))
         moved = dot(jnp.concatenate([high, low], axis=1), z_both) + dot(high, z_low)
         columns = []
-        for t in range(2):
+        for t in range(4):
             real = moved[2 * t * rows : (2 * t + 1) * rows]
             imag = moved[(2 * t + 1) * rows : (2 * t + 2) * rows]
             columns.append(
@@ -162,7 +162,7 @@
             )
         high, low = halves(jnp.concatenate(columns, axis=1))
         moved = dot(y_high, high) + (dot(y_high, low) + dot(y_low, high))
-        for t in range(2):
+        for t in range(4):
             real = moved[:rows, t * LANES : (t + 1) * LANES]
             imag = moved[rows:, t * LANES : (t + 1) * LANES]
             turned_real = real * twist[0] - imag * twist[1]

time: 74.7 us -> 74.3 us (level)
  no operation moved by 1% of the time
where the time goes in v9:
time: 74.3 us; the launch traced here: 73.9 us
  blocking collectives  63.3 us (85%)
  Pallas kernels  8.76 us (12%)
  other arithmetic  1.24 us (2%)
    all_to_all x3, blocking collectives, exchange(): lax.all_to_all(array, names, split_axis=0, concat_axis=0, tiled=True, axi...  63.3 us
    pallas_call x1, Pallas kernels, body(): pl.pallas_call(functools.partial(transform_kernel, points), out_shape=jax...  7.5 us

profile of v9, /device:TPU:1, one launch (start us, length us, event | category | flops | bytes accessed | tf_op | source)
XLA Modules:
  0.0 73.9 jit_solution(16500810748704277249)
XLA Ops:
  0.0 7.5 %transform.1 = f32[32,48,128]{2,1,0:T(8,128)} custom-call(s32[8]{0:T(128)} %valence_ids.1, s32[8]{0:T(128)} %conduct_ids.1, bf16[2,16,128,128]{3,2,1,0:T(8,128)(2,1)} %bitcast.18, bf16[2,16,128,128]{3,2,1,0:T(8,128)(2,1)} %bitcast.19, bf16[2,128,128]{2,1,0:T(8,128)(2,1)} %bitcast.20, s32[80,128]{1,0:T(8,128)} %bitcast.21, ...), custom_call_target="tpu_custom_call" | custom-call | tf_op jit(solution)/shard_map/transform/pallas_call | solution.py:375
  7.5 1.2 %convert_element_type.6 = f16[32,48,128]{2,1,0:T(8,128)(2,1)S(1)} convert(f32[32,48,128]{2,1,0:T(8,128)} %transform.1) | non-fusion elementwise | flops 196608 | bytes 1179648 | tf_op jit(solution)/shard_map/convert_element_type | solution.py:408
  8.7 27.6 %all_to_all.15 = f16[32,48,128]{2,1,0:T(8,128)(2,1)S(1)} all-to-all(f16[32,48,128]{2,1,0:T(8,128)(2,1)S(1)} %convert_element_type.6), channel_id=1, replica_groups={{0,1,2,3,4,5,6,7,8,9,10,11,12,13,14,15,32,33,34,35,36,37,38,39,40,41,42..., dimensions={0} | all-to-all | bytes 786432 | tf_op jit(solution)/shard_map/all_to_all | solution.py:332
  36.3 0.0 copy-start
  36.3 0.1 convert_element_type.7.partial
  36.4 0.6 copy-done
  37.0 0.1 weight.1
  37.1 20.7 %all_to_all.16.gathered = bf16[16,80,128]{2,1,0:T(8,128)(2,1)S(1)} all-to-all(bf16[16,80,128]{2,1,0:T(8,128)(2,1)S(1)} %weight.1), channel_id=1, replica_groups={{0,16,64,80,128,144,192,208,256,272,320,336,384,400,448,464},{32,48,96,..., dimensions={0} | all-to-all | bytes 655360 | tf_op jit(solution)/shard_map/all_to_all | solution.py:332
  57.8 0.4 panel.1
  58.2 15.0 %all_to_all.17.partial = f32[32,2,128]{2,1,0:T(2,128)S(1)} all-to-all(f32[32,2,128]{2,1,0:T(2,128)S(1)} %panel.1), channel_id=1, replica_groups={{0,1,4,5,8,9,12,13,48,49,52,53,56,57,60,61,18,19,22,23,26,27,30,31,34,3..., dimensions={0} | all-to-all | bytes 65536 | tf_op jit(solution)/shard_map/all_to_all | solution.py:332
  73.2 0.7 total.1
Async XLA Ops:
  36.3 0.7 copy-start
